TPU v7x, 128 devices: a whole 4x4x4 slice. The times are simulated.
128 devices in a mesh: outer: 16 (over y_lo, z, core), blk: 8 (over y_hi, x).
Axes of the slice: x: 4, y: 4 (y_hi: 2, y_lo: 2; y = y_hi * 2 + y_lo), z: 4, core: 2. Of those that a mesh axis runs over, the one named last changes fastest.
Arguments:
- image_feats: bfloat16 [16384, 1152], P(('outer', 'blk')), may hold values from -0.29882812 to 0.29882812
- text_feats: bfloat16 [16384, 1152], P(('outer', 'blk')), may hold values from -0.29882812 to 0.29882812
- image_weight: bfloat16 [1152, 1152], replicated, may hold values from -0.1875 to 0.1875
- text_weight: bfloat16 [1152, 1152], replicated, may hold values from -0.1875 to 0.1875
- temper: float32 [1], replicated, may hold values from 5 to 12
- offset: float32 [1], replicated, may hold values from -7 to -5
Outputs:
- image_loss: float32 [16384], P(('outer', 'blk'))
- grad_image: float32 [16384, 1152], P(('outer', 'blk'))
- grad_text: float32 [16384, 1152], P(('outer', 'blk'))
- grad_image_weight: float32 [1152, 1152], replicated
- grad_text_weight: float32 [1152, 1152], replicated
All inputs are finite; a program needn't handle non-finite values.
Results may differ from a plain program's by a relative error of at most 0.017.
Values may be sent and summed in bfloat16 or wider, within the bound.
No kernel may reach another device: no remote copies, remote signals or barrier semaphores. Data moves between devices by JAX's collectives and lax.ppermute only.
A program may use at most 128 MiB of HBM per device.

v0:
```python
import jax
import jax.numpy as jnp
from jax import lax
from jax.sharding import PartitionSpec as P

EPS = 1e-06
HIGH = lax.Precision.HIGHEST


def tower(feats, weight):
    values = feats.astype(jnp.float32)
    centered = values - jnp.mean(values, -1, keepdims=True)
    inverse = lax.rsqrt(jnp.mean(centered * centered, -1, keepdims=True) + EPS)
    normed = centered * inverse
    hidden = normed.astype(jnp.bfloat16)
    proj = jnp.dot(hidden, weight, preferred_element_type=jnp.float32)
    scale = lax.rsqrt(jnp.sum(proj * proj, -1, keepdims=True) + EPS)
    embed = (proj * scale).astype(jnp.bfloat16)
    return (normed, inverse, hidden, proj, scale, embed)


def tower_back(state, weight, grad_embed):
    normed, inverse, hidden, proj, scale, embed = state
    grad_proj = scale * grad_embed - scale * scale * scale * proj * jnp.sum(
        proj * grad_embed, -1, keepdims=True
    )
    grad_weight = jnp.dot(hidden.astype(jnp.float32).T, grad_proj, precision=HIGH)
    grad_hidden = jnp.dot(grad_proj, weight.astype(jnp.float32).T, precision=HIGH)
    centered = grad_hidden - jnp.mean(grad_hidden, -1, keepdims=True)
    grad_feats = inverse * (centered - normed * jnp.mean(grad_hidden * normed, -1, keepdims=True))
    return (grad_feats, grad_weight)


def pair_terms(images, image_ids, texts, text_ids, temper, offset):
    scores = lax.dot_general(
        images, texts, (((1,), (1,)), ((), ())), preferred_element_type=jnp.float32
    )
    logits = temper[0] * scores + offset[0]
    signs = jnp.where(image_ids[:, None] == text_ids[None, :], 1.0, -1.0).astype(jnp.float32)
    flipped = -signs * logits
    loss_rows = jnp.sum(jax.nn.softplus(flipped), 1)
    weights = (-temper[0] * signs * jax.nn.sigmoid(flipped)).astype(jnp.bfloat16)
    return (weights, loss_rows)


def contract_rows(weights, values):
    return lax.dot_general(
        weights, values, (((0,), (0,)), ((), ())), preferred_element_type=jnp.float32
    )


def per_device(image_feats, text_feats, image_weight, text_weight, temper, offset):
    rows = image_feats.shape[0]
    outer_at = lax.axis_index("outer")
    blk_at = lax.axis_index("blk")
    n_blk = lax.axis_size("blk")
    image_state = tower(image_feats, image_weight)
    text_state = tower(text_feats, text_weight)
    img_embed = image_state[5]
    txt_embed = text_state[5]
    near_count = n_blk * rows
    near_ids = outer_at * near_count + jnp.arange(near_count, dtype=jnp.int32)
    near_images = lax.all_gather(img_embed, "blk", axis=0, tiled=True)
    piece = lax.all_gather(txt_embed, "outer", axis=0, tiled=True)
    slot = jnp.arange(piece.shape[0], dtype=jnp.int32)
    weights, loss_rows = pair_terms(
        near_images,
        near_ids,
        piece,
        (slot // rows * n_blk + blk_at) * rows + slot % rows,
        temper,
        offset,
    )
    grad_img = jnp.dot(weights, piece, preferred_element_type=jnp.float32)
    grad_txt = contract_rows(weights, near_images)
    grad_img, image_loss, partial_txt = (grad_img, loss_rows, grad_txt)
    grad_txt = lax.psum_scatter(
        partial_txt.astype(jnp.bfloat16), "outer", scatter_dimension=0, tiled=True
    ).astype(jnp.float32)
    grad_img, image_loss = (
        lax.psum_scatter(
            grad_img.astype(jnp.bfloat16), "blk", scatter_dimension=0, tiled=True
        ).astype(jnp.float32),
        lax.psum_scatter(
            image_loss.astype(jnp.bfloat16), "blk", scatter_dimension=0, tiled=True
        ).astype(jnp.float32),
    )
    grad_image, image_part = tower_back(image_state, image_weight, grad_img)
    grad_text, text_part = tower_back(text_state, text_weight, grad_txt)
    grad_image_weight, grad_text_weight = lax.psum((image_part, text_part), ("outer", "blk"))
    return (image_loss, grad_image, grad_text, grad_image_weight, grad_text_weight)


def solution(mesh):
    in_specs = (P(("outer", "blk"), None), P(("outer", "blk"), None), P(), P(), P(), P())
    out_specs = (
        P(("outer", "blk")),
        P(("outer", "blk"), None),
        P(("outer", "blk"), None),
        P(),
        P(),
    )
    return jax.shard_map(
        per_device, mesh=mesh, in_specs=in_specs, out_specs=out_specs, check_vma=False
    )
```

profile of v0, /device:TPU:1, one launch (start us, length us, event | category | flops | bytes accessed | tf_op | source)
XLA Modules:
  0.0 470.2 jit_solution(15027583907702026606)
XLA Ops:
  7.2 0.0 copy-start
  7.2 0.0 all-gather.3.cloned.1.call-start
  7.2 1.2 convert_reduce_fusion.1
  8.5 1.2 fusion.21
  9.7 1.7 multiply_reduce_fusion.1
  11.4 0.6 multiply_multiply_fusion.1
  12.0 0.8 multiply_convert_fusion.1
  12.8 0.0 all-gather.3.cloned.1.call-update
  12.8 0.0 all-gather.5.cloned.1.call-start
  12.9 0.1 convert_reduce_fusion
  13.0 0.2 fusion.17
  13.2 2.5 multiply_reduce_fusion
  15.7 0.0 copy-start.1
  15.7 0.6 multiply_multiply_fusion
  16.3 0.2 copy-done.1
  16.6 0.3 copy-done.10
  16.8 0.8 multiply_convert_fusion
  17.6 0.0 all-gather.5.cloned.1.call-update
  17.7 0.0 reduce-scatter.3.cloned.1.call-start
  19.0 53.0 %all-gather.3.cloned.1.call-done = bf16[1024,1152]{1,0:T(8,128)(2,1)} async-done(((bf16[128,1152]{1,0:T(8,128)(2,1)}), bf16[1024,1152]{1,0:T(8,128)(2,1)}) %all-gather.3.cloned.1.call-update) | async-done | bytes 2359312 | tf_op jit(solution)/shard_map/all_gather | solution.py:63
  72.0 41.2 %all-gather.5.cloned.1.call-done = bf16[2048,1152]{1,0:T(8,128)(2,1)} async-done(((bf16[128,1152]{1,0:T(8,128)(2,1)}), bf16[2048,1152]{1,0:T(8,128)(2,1)}) %all-gather.5.cloned.1.call-update) | async-done | bytes 4718608 | tf_op jit(solution)/shard_map/all_gather | solution.py:64
  113.2 15.3 %fusion.2 = (bf16[1024,2048]{1,0:T(8,128)(2,1)S(1)}, bf16[1024]{0:T(1024)(128)(2,1)}) fusion(f32[]{:T(128)S(6)} %neg.15, f32[]{:T(128)} %bitcast.15, f32[]{:T(128)} %bitcast.13, s32[2048]{0:T(1024)S(1)} %fusion.55, s32[1024]{0:T(1024)S(1)} %iota_add_fusion, bf16[1024,1152]{1,0:T(8,128)(2,1)} %all-gather.3.cloned.1.call-done, ...), kind=kOutput, calls=%fused_computation.5 | convolution fusion | flops 4871683072 | bytes 11286540 | tf_op jit(solution)/shard_map/dot_general | solution.py:35
  128.5 2.0 copy-done.14
  130.5 6.8 %convolution_convert_fusion.1 = bf16[1024,1152]{1,0:T(8,128)(2,1)} fusion(bf16[1024,2048]{1,0:T(8,128)(2,1)S(1)} %get-tuple-element.11, bf16[2048,1152]{1,0:T(8,128)(2,1)S(1)} %copy-done.13), kind=kOutput, calls=%fused_computation.8 | convolution fusion | flops 4833017856 | bytes 11272192 | tf_op jit(solution)/shard_map/dot_general | solution.py:74
  137.3 0.0 reduce-scatter.3.cloned.1.call-update
  137.3 0.2 reduce-scatter.5.cloned.1.call-start
  137.6 9.6 %convolution_convert_fusion = bf16[2048,1152]{1,0:T(8,128)(2,1)} fusion(bf16[1024,2048]{1,0:T(8,128)(2,1)} %copy-done.14, bf16[1024,1152]{1,0:T(8,128)(2,1)} %all-gather.3.cloned.1.call-done), kind=kOutput, calls=%fused_computation.7 | convolution fusion | flops 4834197504 | bytes 11272192 | tf_op jit(solution)/shard_map/dot_general | solution.py:47
  147.2 0.0 reduce-scatter.5.cloned.1.call-update
  147.2 0.0 all-reduce.4.cloned.1.call-start
  147.2 65.7 %reduce-scatter.3.cloned.1.call-done = bf16[128,1152]{1,0:T(8,128)(2,1)} async-done(((bf16[1024,1152]{1,0:T(8,128)(2,1)}), bf16[128,1152]{1,0:T(8,128)(2,1)}) %reduce-scatter.3.cloned.1.call-update) | async-done | bytes 294928 | tf_op jit(solution)/shard_map/reduce_scatter | solution.py:81
  212.9 1.1 fusion.23
  214.1 0.6 copy-done.12
  214.6 5.8 %fusion.30 = f32[1152,1152]{1,0:T(8,128)} fusion(bf16[128,1152]{1,0:T(8,128)(2,1)} %reduce-scatter.3.cloned.1.call-done, f32[128,1152]{1,0:T(8,128)S(1)} %get-tuple-element.18, f32[128]{0:T(128)S(1)} %fusion.23, f32[128]{0:T(128)} %get-tuple-element.15, f32[128]{0:T(128)} %copy-done.9, bf16[128,1152]{1,0:T(8,128)(2,1)S(1)} %copy-done.3, ...), kind=kOutput, calls=%fused_computation.45 | convolution fusion | flops 2039758848 | bytes 6490624 | tf_op jit(solution)/shard_map/dot_general | solution.py:27
  220.4 59.4 %reduce-scatter.5.cloned.1.call-done = bf16[128,1152]{1,0:T(8,128)(2,1)} async-done(((bf16[2048,1152]{1,0:T(8,128)(2,1)}), bf16[128,1152]{1,0:T(8,128)(2,1)}) %reduce-scatter.5.cloned.1.call-update) | async-done | bytes 294928 | tf_op jit(solution)/shard_map/reduce_scatter | solution.py:77
  279.8 1.3 fusion.25
  281.1 0.5 copy-done.11
  281.6 6.0 %fusion.26 = f32[1152,1152]{1,0:T(8,128)} fusion(bf16[128,1152]{1,0:T(8,128)(2,1)} %reduce-scatter.5.cloned.1.call-done, f32[128,1152]{1,0:T(8,128)} %copy-done.1, f32[128]{0:T(128)S(1)} %fusion.25, f32[128]{0:T(128)} %get-tuple-element.13, f32[128]{0:T(128)} %copy-done.10, bf16[128,1152]{1,0:T(8,128)(2,1)} %param.7, f32[128]{0:T(128)S(1)} %add_rsqrt_fusion.1, ...), kind=kOutput, calls=%fused_computation.43 | convolution fusion | flops 2039758848 | bytes 6490624 | tf_op jit(solution)/shard_map/dot_general | solution.py:27
  287.6 0.0 all-reduce.4.cloned.1.call-update
  287.7 1.2 dynamic-slice
  289.6 21.7 %all-reduce = bf16[1024]{0:T(1024)(128)(2,1)} all-reduce(bf16[1024]{0:T(1024)(128)(2,1)} %get-tuple-element.12), channel_id=2, replica_groups=mesh['outer'=16,'blk'=8] {'blk'}, use_global_device_ids=true, to_apply=%region_7.8.clone | all-reduce | flops 1024 | bytes 4096
  311.3 1.4 dynamic-slice_convert_fusion
  312.7 3.5 fusion.64
  316.2 1.1 fusion.20
  317.3 3.3 fusion.63
  320.6 1.1 fusion.16
  321.7 134.3 %all-reduce.4.cloned.1.call-done = (f32[1152,1152]{1,0:T(8,128)}, f32[1152,1152]{1,0:T(8,128)}) async-done(((f32[1152,1152]{1,0:T(8,128)}, f32[1152,1152]{1,0:T(8,128)}), (f32[1152,1152]{1,0:T(8,128)}, f32[1152,1152]{1,0:T(8,128)})) %all-reduce.4.cloned.1.call-update) | async-done | bytes 10616848 | tf_op jit(solution)/shard_map/psum | solution.py:90
  456.0 5.4 %copy.15 = f32[1152,1152]{1,0:T(8,128)} copy(f32[1152,1152]{1,0:T(8,128)} %get-tuple-element.30) | data formatting | bytes 10616832
  461.3 2.4 copy.16
  (31 shorter events, 0.1 us)
Async XLA Ops:
  7.2 2.5 copy-start
  7.2 5.7 %copy-start.4 = (bf16[128,1152]{1,0:T(8,128)(2,1)S(1)}, bf16[128,1152]{1,0:T(8,128)(2,1)}, u32[]{:S(2)}) copy-start(bf16[128,1152]{1,0:T(8,128)(2,1)} %param.7) | copy-start | bytes 884740
  7.2 64.8 %all-gather.3.cloned.1.call-start = ((), (), s32[]{:S(2)}) async-start(), calls=%async_computation.2 | async-start | bytes 2654208 | tf_op jit(solution)/shard_map/all_gather | solution.py:63
  11.9 0.9 copy-start.9
  12.8 100.4 %all-gather.5.cloned.1.call-start = ((), (), s32[]{:S(2)}) async-start(), calls=%async_computation.3 | async-start | bytes 5013504 | tf_op jit(solution)/shard_map/all_gather | solution.py:64
  15.7 0.8 copy-start.1
  16.3 0.5 copy-start.10
  17.7 195.3 %reduce-scatter.3.cloned.1.call-start = ((), (), s32[]{:S(2)}) async-start(), calls=%async_computation.4 | async-start | bytes 2654208 | tf_op jit(solution)/shard_map/reduce_scatter | solution.py:81
  113.2 17.3 %copy-start.13 = (bf16[2048,1152]{1,0:T(8,128)(2,1)S(1)}, bf16[2048,1152]{1,0:T(8,128)(2,1)}, u32[]{:S(2)}) copy-start(bf16[2048,1152]{1,0:T(8,128)(2,1)} %all-gather.5.cloned.1.call-done) | copy-start | bytes 14155780
  128.5 2.0 copy-start.14
  137.3 142.5 %reduce-scatter.5.cloned.1.call-start = ((), (), s32[]{:S(2)}) async-start(), calls=%async_computation.5 | async-start | bytes 5013504 | tf_op jit(solution)/shard_map/reduce_scatter | solution.py:77
  147.1 67.5 %copy-start.3 = (bf16[128,1152]{1,0:T(8,128)(2,1)S(1)}, bf16[128,1152]{1,0:T(8,128)(2,1)}, u32[]{:S(2)}) copy-start(bf16[128,1152]{1,0:T(8,128)(2,1)} %param.6) | copy-start | bytes 884740
  147.2 308.8 %all-reduce.4.cloned.1.call-start = ((), (), s32[]{:S(2)}) async-start(), calls=%async_computation.6 | async-start | bytes 21233664 | tf_op jit(solution)/shard_map/psum | solution.py:90
  214.0 0.6 copy-start.12
  281.1 0.5 copy-start.11
  311.3 6.1 %copy-start.2 = (f32[128,1152]{1,0:T(8,128)S(1)}, f32[128,1152]{1,0:T(8,128)}, u32[]{:S(2)}) copy-start(f32[128,1152]{1,0:T(8,128)} %copy-done.1) | copy-start | bytes 1769476
  311.3 6.1 %copy-start.5 = (bf16[128,1152]{1,0:T(8,128)(2,1)S(1)}, bf16[128,1152]{1,0:T(8,128)(2,1)}, u32[]{:S(2)}) copy-start(bf16[128,1152]{1,0:T(8,128)(2,1)} %param.7) | copy-start | bytes 884740
  311.3 6.1 %copy-start.6 = (bf16[1152,1152]{1,0:T(8,128)(2,1)S(1)}, bf16[1152,1152]{1,0:T(8,128)(2,1)}, u32[]{:S(2)}) copy-start(bf16[1152,1152]{1,0:T(8,128)(2,1)} %param.9) | copy-start | bytes 7962628
  311.3 6.1 %copy-start.8 = (bf16[128,1152]{1,0:T(8,128)(2,1)S(1)}, bf16[128,1152]{1,0:T(8,128)(2,1)}, u32[]{:S(2)}) copy-start(bf16[128,1152]{1,0:T(8,128)(2,1)} %reduce-scatter.5.cloned.1.call-done) | copy-start | bytes 884740
  456.0 5.4 %copy-start.7 = (f32[1152,1152]{1,0:T(8,128)S(1)}, f32[1152,1152]{1,0:T(8,128)}, u32[]{:S(2)}) copy-start(f32[1152,1152]{1,0:T(8,128)} %get-tuple-element.31) | copy-start | bytes 15925252
Sparse Core Ops, SparseCore 0:
  12.9 59.0 all-gather.2
  74.3 38.8 all-gather.4
  137.4 75.4 reduce-scatter.2
  215.9 63.8 reduce-scatter.4
  287.8 168.1 all-reduce.3
where the time goes:
time: 471 us; the launch traced here: 470 us
  waiting for transfers between devices  354 us (75%)
  matrix products  54.5 us (12%)
  blocking collectives  21.7 us (5%)
  between operations  15.9 us (3%)
  local copies, waits for them, and re-layouts  12.7 us (3%)
  other arithmetic  11.5 us (2%)
    psum x1, waiting for transfers between devices, per_device(): lax.psum((image_part, text_part), ('outer', 'blk'))  134 us
    reduce_scatter x1, waiting for transfers between devices, per_device(): lax.psum_scatter(grad_img.astype(jnp.bfloat16), 'blk', scatter_dimension=...  65.7 us
    reduce_scatter x1, waiting for transfers between devices, per_device(): lax.psum_scatter(partial_txt.astype(jnp.bfloat16), 'outer', scatter_dimen...  59.4 us
    all_gather x1, waiting for transfers between devices, per_device(): near_images = lax.all_gather(img_embed, 'blk', axis=0, tiled=True)  53 us
    all_gather x1, waiting for transfers between devices, per_device(): piece = lax.all_gather(txt_embed, 'outer', axis=0, tiled=True)  41.2 us
    unnamed x1, blocking collectives  21.7 us
    dot_general x1, matrix products, pair_terms(): lax.dot_general(images, texts, (((1,), (1,)), ((), ())), preferred_elemen...  15.3 us
    unnamed x33, local copies, waits for them, and re-layouts  12.7 us
  transfers between devices with their start and end apart: 5, of which 5 were waited for; matrix products, arithmetic and copies ran while one was open for 7% of the time, Pallas kernels for 0%

commit v1 on v0

v1 whole, which is shorter than its diff:
```python
import jax
import jax.numpy as jnp
from jax import lax
from jax.sharding import Mesh, PartitionSpec as P

EPS = 1e-06
BF = jnp.bfloat16
F32 = jnp.float32
AXES = ("yl", "z", "c", "yh", "x")


def split_mesh(mesh):
    return Mesh(mesh.devices.reshape(2, 4, 2, 2, 4), AXES)


def tower(feats, weight):
    values = feats.astype(F32)
    centered = values - jnp.mean(values, -1, keepdims=True)
    inverse = lax.rsqrt(jnp.mean(centered * centered, -1, keepdims=True) + EPS)
    normed = centered * inverse
    hidden = normed.astype(BF)
    proj = jnp.dot(hidden, weight, preferred_element_type=F32)
    scale = lax.rsqrt(jnp.sum(proj * proj, -1, keepdims=True) + EPS)
    embed = (proj * scale).astype(BF)
    return (normed, inverse, hidden, proj, scale, embed)


def back_proj(state, grad_embed):
    normed, inverse, hidden, proj, scale, embed = state
    return scale * grad_embed - scale * scale * scale * proj * jnp.sum(proj * grad_embed, -1, keepdims=True)


def back_feats(state, weight, grad_proj):
    normed, inverse, hidden, proj, scale, embed = state
    grad_hidden = lax.dot_general(grad_proj, weight, (((1,), (1,)), ((), ())), preferred_element_type=F32)
    centered = grad_hidden - jnp.mean(grad_hidden, -1, keepdims=True)
    return inverse * (centered - normed * jnp.mean(grad_hidden * normed, -1, keepdims=True))


def fetch(block, axis, step):
    return lax.ppermute(block, axis, [(i, (i - step) % 4) for i in range(4)])


def give(block, axis, step):
    return lax.ppermute(block, axis, [(i, (i + step) % 4) for i in range(4)])


def swap(block, axis):
    return lax.ppermute(block, axis, [(0, 1), (1, 0)])


STEPS = (1, 3, 2)


def gather8(block, ring, pair):
    other = swap(block, pair)
    near = [block] + [fetch(block, ring, s) for s in STEPS]
    far = [other] + [fetch(other, ring, s) for s in STEPS]
    return near + far


def scatter8(parts, ring, pair):
    def ring_sum(four):
        total = four[0].astype(F32)
        for s, part in zip(STEPS, four[1:]):
            total = total + give(part, ring, s).astype(F32)
        return total

    far = swap(ring_sum(parts[4:]).astype(BF), pair)
    return ring_sum(parts[:4]) + far.astype(F32)


def reduce_weights(part):
    rows, cols = part.shape
    mine = lax.all_to_all(part.astype(BF).reshape(16, rows // 16, cols), ("z", "x"), 0, 0, tiled=True)
    mine = jnp.sum(mine.astype(F32), 0).astype(BF)
    total = mine.astype(F32)
    for s in STEPS:
        total = total + lax.ppermute(mine, ("yl", "yh"), y_pairs(s)).astype(F32)
    total = total.astype(BF)
    full = lax.all_to_all(jnp.broadcast_to(total[None], (16,) + total.shape), ("z", "x"), 0, 0, tiled=True)
    return full.reshape(rows, cols)


def y_pairs(step):
    at = lambda y: (y % 2) * 2 + y // 2
    return [(at(y), at((y + step) % 4)) for y in range(4)]


def per_device(image_feats, text_feats, image_weight, text_weight, temper, offset):
    rows = image_feats.shape[0]
    core = lax.axis_index("c")
    image_state = tower(image_feats, image_weight)
    text_state = tower(text_feats, text_weight)
    images = jnp.concatenate(gather8(image_state[5], "x", "yh"))
    texts_same = jnp.concatenate(gather8(text_state[5], "z", "yl"))
    texts = jnp.concatenate([texts_same, swap(texts_same, "c")])
    scores = lax.dot_general(images, texts, (((1,), (1,)), ((), ())), preferred_element_type=F32)
    logits = temper[0] * scores + offset[0]
    near = lax.broadcasted_iota(jnp.int32, logits.shape, 0)
    signs = jnp.where(
        (near == lax.broadcasted_iota(jnp.int32, logits.shape, 1)) & (near < rows), 1.0, -1.0
    ).astype(F32)
    flipped = -signs * logits
    loss_rows = jnp.sum(jax.nn.softplus(flipped), 1)
    weights = (-temper[0] * signs * jax.nn.sigmoid(flipped)).astype(BF)
    grad_img = jnp.dot(weights, texts, preferred_element_type=F32).astype(BF)
    grad_txt = lax.dot_general(weights, images, (((0,), (0,)), ((), ())), preferred_element_type=F32)
    half = grad_txt.shape[0] // 2
    grad_txt = (grad_txt[:half] + swap(grad_txt[half:].astype(BF), "c").astype(F32)).astype(BF)
    grad_img = scatter8(jnp.split(grad_img, 8), "x", "yh")
    grad_txt = scatter8(jnp.split(grad_txt, 8), "z", "yl")
    loss8 = lax.all_to_all(loss_rows.reshape(8, rows)[reorder()], ("yh", "x"), 0, 0, tiled=True)
    image_loss = jnp.sum(loss8, 0)
    image_gp = back_proj(image_state, grad_img).astype(BF)
    text_gp = back_proj(text_state, grad_txt).astype(BF)
    image_pack = jnp.concatenate([image_state[2], image_gp])
    text_pack = jnp.concatenate([text_state[2], text_gp])
    keep = jnp.where(core == 0, image_pack, text_pack)
    got = swap(jnp.where(core == 0, text_pack, image_pack), "c")
    hidden = jnp.concatenate([keep[:rows], got[:rows]])
    grad_proj = jnp.concatenate([keep[rows:], got[rows:]])
    part = lax.dot_general(hidden, grad_proj, (((0,), (0,)), ((), ())), preferred_element_type=F32)
    mine = reduce_weights(part)
    other = swap(mine, "c")
    grad_image_weight = jnp.where(core == 0, mine, other).astype(F32)
    grad_text_weight = jnp.where(core == 0, other, mine).astype(F32)
    grad_image = back_feats(image_state, image_weight, image_gp)
    grad_text = back_feats(text_state, text_weight, text_gp)
    return (image_loss, grad_image, grad_text, grad_image_weight, grad_text_weight)


def reorder():
    yh, x = lax.axis_index("yh"), lax.axis_index("x")
    owner = jnp.arange(8)
    step = (owner % 4 - x) % 4
    place = jnp.where(step == 2, 3, jnp.where(step == 3, 2, step))
    return (owner // 4 != yh).astype(jnp.int32) * 4 + place


def solution(mesh):
    rows = P(AXES, None)
    in_specs = (rows, rows, P(), P(), P(), P())
    out_specs = (P(AXES), rows, rows, P(), P())
    return jax.shard_map(
        per_device, mesh=split_mesh(mesh), in_specs=in_specs, out_specs=out_specs, check_vma=False
    )
```

time: 471 us -> 286 us (0.61)
  waiting for transfers between devices: 354 us -> 65.6 us
  blocking collectives: 21.7 us -> 84 us
  starting transfers between devices: 0.39 us -> 49.8 us
  matrix products: 54.5 us -> 32.3 us
  other arithmetic: 11.5 us -> 28.4 us
  between operations: 15.9 us -> 2.33 us
  local copies, waits for them, and re-layouts: 12.7 us -> 23.2 us
    psum x1 -> x0, waiting for transfers between devices: 134 us -> none  [per_device(): lax.psum((image_part, text_part), ('outer', 'blk'))]
    reduce_scatter x2 -> x0, waiting for transfers between devices: 125 us -> none  [the longest x1 65.7 us: per_device(): lax.psum_scatter(grad_img.astype(jnp.bfloat16), 'blk', scatter_dimension=...]
    all_gather x2 -> x0, waiting for transfers between devices: 94.1 us -> none  [the longest x1 53 us: per_device(): near_images = lax.all_gather(img_embed, 'blk', axis=0, tiled=True)]
    all_to_all x0 -> x3, blocking collectives: none -> 84 us  [the longest x1 37.3 us: reduce_weights(): lax.all_to_all(part.astype(BF).reshape(16, rows // 16, cols), ('z', 'x'),...]
    ppermute x0 -> x35, waiting for transfers between devices: none -> 65.6 us  [the longest x12 30.8 us: give(): return lax.ppermute(block, axis, [(i, (i + step) % 4) for i in range(4)])]
    ppermute x0 -> x35, starting transfers between devices: none -> 49.8 us  [the longest x12 18 us: fetch(): return lax.ppermute(block, axis, [(i, (i - step) % 4) for i in range(4)])]
    dot_general x9 -> x8, matrix products: 54.5 us -> 32.3 us  [the longest x1 14.4 us: per_device(): lax.dot_general(images, texts, (((1,), (1,)), ((), ())), preferred_elemen...]
    unnamed x1 -> x0, blocking collectives: 21.7 us -> none
  transfers between devices with their start and end apart: 5 -> 35, of which waited for: 5 -> 24; matrix products, arithmetic and copies ran while one was open for 7% -> 13% of each run, Pallas kernels for 0% -> 0%
where the time goes in v1:
time: 286 us
  blocking collectives  84 us (29%)
  waiting for transfers between devices  65.6 us (23%)
  starting transfers between devices  49.8 us (17%)
  matrix products  32.3 us (11%)
  other arithmetic  28.4 us (10%)
  local copies, waits for them, and re-layouts  23.2 us (8%)
    all_to_all x1, blocking collectives, reduce_weights(): lax.all_to_all(part.astype(BF).reshape(16, rows // 16, cols), ('z', 'x'),...  37.3 us
    all_to_all x1, blocking collectives, reduce_weights(): lax.all_to_all(jnp.broadcast_to(total[None], (16,) + total.shape), ('z',...  36.5 us
    ppermute x12, waiting for transfers between devices, give(): return lax.ppermute(block, axis, [(i, (i + step) % 4) for i in range(4)])  30.8 us
    ppermute x12, waiting for transfers between devices, fetch(): return lax.ppermute(block, axis, [(i, (i - step) % 4) for i in range(4)])  20.8 us
    ppermute x12, starting transfers between devices, fetch(): return lax.ppermute(block, axis, [(i, (i - step) % 4) for i in range(4)])  18 us
    ppermute x8, starting transfers between devices, swap(): return lax.ppermute(block, axis, [(0, 1), (1, 0)])  17.9 us
    unnamed x63, local copies, waits for them, and re-layouts  14.9 us
    dot_general x1, matrix products, per_device(): lax.dot_general(images, texts, (((1,), (1,)), ((), ())), preferred_elemen...  14.4 us
  transfers between devices with their start and end apart: 35, of which 24 were waited for; matrix products, arithmetic and copies ran while one was open for 13% of the time, Pallas kernels for 0%

profile of v1, /device:TPU:1, one launch (start us, length us, event | category | flops | bytes accessed | tf_op | source)
XLA Modules:
  0.0 285.6 jit_solution(3302466575695501116)
XLA Ops:
  4.3 2.5 multiply_reduce_fusion.2
  8.3 4.6 %collective-permute-start.7 = (bf16[128,1152]{1,0:T(8,128)(2,1)S(1)}, bf16[128,1152]{1,0:T(8,128)(2,1)S(1)}, u32[]{:S(2)}, u32[]{:S(2)}) collective-permute-start(bf16[128,1152]{1,0:T(8,128)(2,1)S(1)} %get-tuple-element.10), channel_id=1, source_target_pairs={{0,48},{16,0},{32,16},{48,32},{1,49},{17,1},{33,17},{49,33},{2,50}... | collective-permute-start | bytes 884744 | tf_op jit(solution)/shard_map/ppermute | solution.py:41
  17.5 3.7 %collective-permute-done.10 = bf16[128,1152]{1,0:T(8,128)(2,1)S(1)} collective-permute-done((bf16[128,1152]{1,0:T(8,128)(2,1)S(1)}, bf16[128,1152]{1,0:T(8,128)(2,1)S(1)}, u32[]{:S(2)}, u32[]{:S(2)}) %collective-permute-start.10) | collective-permute-done | bytes 294944 | tf_op jit(solution)/shard_map/ppermute | solution.py:49
  21.2 1.7 collective-permute-start.11
  23.2 1.6 collective-permute-done.7
  28.2 9.2 %collective-permute-done.11 = bf16[128,1152]{1,0:T(8,128)(2,1)S(1)} collective-permute-done((bf16[128,1152]{1,0:T(8,128)(2,1)S(1)}, bf16[128,1152]{1,0:T(8,128)(2,1)S(1)}, u32[]{:S(2)}, u32[]{:S(2)}) %collective-permute-start.11) | collective-permute-done | bytes 294944 | tf_op jit(solution)/shard_map/ppermute | solution.py:41
  38.2 2.7 collective-permute-done.12
  42.4 1.6 collective-permute-start.14
  45.0 2.9 %collective-permute-start.3 = (bf16[128,1152]{1,0:T(8,128)(2,1)}, bf16[128,1152]{1,0:T(8,128)(2,1)}, u32[]{:S(2)}, u32[]{:S(2)}) collective-permute-start(bf16[128,1152]{1,0:T(8,128)(2,1)} %get-tuple-element.12), channel_id=1, source_target_pairs={{0,4},{4,0},{1,5},{5,1},{2,6},{6,2},{3,7},{7,3},{8,12},{12,8},{9,1... | collective-permute-start | bytes 884744 | tf_op jit(solution)/shard_map/ppermute | solution.py:49
  47.9 2.5 collective-permute-start
  50.4 1.7 collective-permute-start.2
  53.9 2.5 collective-permute-start.4
  56.4 1.7 constant_dynamic-update-slice_fusion.6
  59.4 3.3 %collective-permute-start.6 = (bf16[128,1152]{1,0:T(8,128)(2,1)}, bf16[128,1152]{1,0:T(8,128)(2,1)S(1)}, u32[]{:S(2)}, u32[]{:S(2)}) collective-permute-start(bf16[128,1152]{1,0:T(8,128)(2,1)} %collective-permute-done.3), channel_id=1, source_target_pairs={{0,2},{1,3},{2,0},{3,1},{4,6},{5,7},{6,4},{7,5},{8,10},{9,11},{10,... | collective-permute-start | bytes 884744 | tf_op jit(solution)/shard_map/ppermute | solution.py:41
  62.6 1.7 constant_dynamic-update-slice_fusion.5
  64.3 1.7 constant_dynamic-update-slice_fusion.4
  66.0 1.7 constant_dynamic-update-slice_fusion.3
  67.7 1.7 collective-permute-done.4
  70.2 4.1 %collective-permute-done.5 = bf16[128,1152]{1,0:T(8,128)(2,1)S(1)} collective-permute-done((bf16[128,1152]{1,0:T(8,128)(2,1)}, bf16[128,1152]{1,0:T(8,128)(2,1)S(1)}, u32[]{:S(2)}, u32[]{:S(2)}) %collective-permute-start.5) | collective-permute-done | bytes 294944 | tf_op jit(solution)/shard_map/ppermute | solution.py:41
  75.7 3.4 %constant_dynamic-update-slice_fusion.16 = bf16[2048,1152]{1,0:T(8,128)(2,1)} fusion(bf16[2048,1152]{1,0:T(8,128)(2,1)} %copy-done.17, bf16[1024,1152]{1,0:T(8,128)(2,1)} %collective-permute-done.14), kind=kLoop, calls=%fused_computation.78 | loop fusion | bytes 4718592 | tf_op jit(solution)/shard_map/concatenate | solution.py:97
  79.1 14.4 %fusion.2 = (bf16[1024,2048]{1,0:T(8,128)(2,1)S(1)}, f32[1024]{0:T(1024)S(1)}) fusion(f32[]{:T(128)S(6)} %neg.15, f32[]{:T(128)} %bitcast.28, f32[]{:T(128)} %bitcast.26, pred[1024]{0:T(1024)(128)(4,1)S(1)} %iota_compare_fusion.1, bf16[1024,1152]{1,0:T(8,128)(2,1)S(1)} %copy-done.16, bf16[2048,1152]{1,0:T(8,128)(2,1)} %constant_dynamic-update-slice_fusion.16), kind=kOutput, calls=%fused_computation.6 | convolution fusion | flops 4873780224 | bytes 11277324 | tf_op jit(solution)/shard_map/dot_general | solution.py:98
  93.5 5.9 %fusion.41 = f32[2048,1152]{1,0:T(8,128)S(1)} fusion(bf16[1024,2048]{1,0:T(8,128)(2,1)S(1)} %get-tuple-element.13, bf16[1024,1152]{1,0:T(8,128)(2,1)S(1)} %copy-done.16), kind=kOutput, calls=%fused_computation.124 | convolution fusion | flops 4831838208 | bytes 15990784 | tf_op jit(solution)/shard_map/dot_general | solution.py:108
  99.7 6.0 %collective-permute-start.22 = (bf16[1024,1152]{1,0:T(8,128)(2,1)S(1)}, bf16[1024,1152]{1,0:T(8,128)(2,1)S(1)}, u32[]{:S(2)}, u32[]{:S(2)}) collective-permute-start(bf16[1024,1152]{1,0:T(8,128)(2,1)S(1)} %slice.37), channel_id=1, source_target_pairs={{0,8},{8,0},{1,9},{9,1},{2,10},{10,2},{3,11},{11,3},{4,12},{12,4},... | collective-permute-start | bytes 7077896 | tf_op jit(solution)/shard_map/ppermute | solution.py:49
  105.7 5.8 %convolution_convert_fusion.1 = bf16[1024,1152]{1,0:T(8,128)(2,1)S(1)} fusion(bf16[1024,2048]{1,0:T(8,128)(2,1)S(1)} %get-tuple-element.13, bf16[2048,1152]{1,0:T(8,128)(2,1)S(1)} %copy-done.18), kind=kOutput, calls=%fused_computation.14 | convolution fusion | flops 4833017856 | bytes 11272192 | tf_op jit(solution)/shard_map/dot_general | solution.py:107
  114.1 2.9 %collective-permute-start.17 = (bf16[128,1152]{1,0:T(8,128)(2,1)S(1)}, bf16[128,1152]{1,0:T(8,128)(2,1)}, u32[]{:S(2)}, u32[]{:S(2)}) collective-permute-start(bf16[128,1152]{1,0:T(8,128)(2,1)S(1)} %get-tuple-element.27), channel_id=1, source_target_pairs={{0,2},{1,3},{2,0},{3,1},{4,6},{5,7},{6,4},{7,5},{8,10},{9,11},{10,... | collective-permute-start | bytes 884744 | tf_op jit(solution)/shard_map/ppermute | solution.py:45
  117.0 3.7 %collective-permute-done.20 = bf16[128,1152]{1,0:T(8,128)(2,1)S(1)} collective-permute-done((bf16[128,1152]{1,0:T(8,128)(2,1)S(1)}, bf16[128,1152]{1,0:T(8,128)(2,1)S(1)}, u32[]{:S(2)}, u32[]{:S(2)}) %collective-permute-start.20) | collective-permute-done | bytes 294944 | tf_op jit(solution)/shard_map/ppermute | solution.py:45
  121.4 5.8 %collective-permute-done.19 = bf16[128,1152]{1,0:T(8,128)(2,1)S(1)} collective-permute-done((bf16[128,1152]{1,0:T(8,128)(2,1)S(1)}, bf16[128,1152]{1,0:T(8,128)(2,1)S(1)}, u32[]{:S(2)}, u32[]{:S(2)}) %collective-permute-start.19) | collective-permute-done | bytes 294944 | tf_op jit(solution)/shard_map/ppermute | solution.py:45
  127.1 2.6 collective-permute-start.15
  129.7 1.9 collective-permute-done.18
  136.6 2.0 collective-permute-done.16
  138.6 2.3 collective-permute-done.15
  142.3 1.8 multiply_reduce_fusion.1
  145.7 4.3 %collective-permute-done.27 = bf16[128,1152]{1,0:T(8,128)(2,1)} collective-permute-done((bf16[128,1152]{1,0:T(8,128)(2,1)}, bf16[128,1152]{1,0:T(8,128)(2,1)}, u32[]{:S(2)}, u32[]{:S(2)}) %collective-permute-start.27) | collective-permute-done | bytes 294944 | tf_op jit(solution)/shard_map/ppermute | solution.py:45
  150.0 3.8 %collective-permute-done.26 = bf16[128,1152]{1,0:T(8,128)(2,1)} collective-permute-done((bf16[128,1152]{1,0:T(8,128)(2,1)}, bf16[128,1152]{1,0:T(8,128)(2,1)}, u32[]{:S(2)}, u32[]{:S(2)}) %collective-permute-start.26) | collective-permute-done | bytes 294944 | tf_op jit(solution)/shard_map/ppermute | solution.py:45
  155.2 1.6 collective-permute-start.29
  156.8 1.6 subtract_convert_fusion.1
  158.4 4.2 %collective-permute-done.24 = bf16[128,1152]{1,0:T(8,128)(2,1)S(1)} collective-permute-done((bf16[128,1152]{1,0:T(8,128)(2,1)}, bf16[128,1152]{1,0:T(8,128)(2,1)S(1)}, u32[]{:S(2)}, u32[]{:S(2)}) %collective-permute-start.24) | collective-permute-done | bytes 294944 | tf_op jit(solution)/shard_map/ppermute | solution.py:45
  162.6 2.7 collective-permute-done.23
  172.7 37.3 %all_to_all.19 = bf16[16,72,1152]{2,1,0:T(8,128)(2,1)} all-to-all(bf16[16,72,1152]{2,1,0:T(8,128)(2,1)S(1)} %bitcast.29), channel_id=1, replica_groups=mesh['yl'=2,'z'=4,'c'=2,'yh'=2,'x'=4] {'z','x'}, dimensions={0} | all-to-all | bytes 5308416 | tf_op jit(solution)/shard_map/all_to_all | solution.py:75
  210.0 2.2 reduce_sum.152
  212.2 2.5 collective-permute-start.33
  216.1 1.8 collective-permute-done.33
  217.9 3.1 %collective-permute-done.32 = bf16[72,1152]{1,0:T(8,128)(2,1)S(1)} collective-permute-done((bf16[72,1152]{1,0:T(8,128)(2,1)S(1)}, bf16[72,1152]{1,0:T(8,128)(2,1)S(1)}, u32[]{:S(2)}, u32[]{:S(2)}) %collective-permute-start.32) | collective-permute-done | bytes 165920 | tf_op jit(solution)/shard_map/ppermute | solution.py:79
  221.0 2.0 collective-permute-done.31
  223.3 36.5 %all_to_all.20 = bf16[16,72,1152]{2,1,0:T(8,128)(2,1)} all-to-all(bf16[16,72,1152]{2,1,0:T(8,128)(2,1)S(1)} %broadcast_in_dim.15), channel_id=1, replica_groups=mesh['yl'=2,'z'=4,'c'=2,'yh'=2,'x'=4] {'z','x'}, dimensions={0} | all-to-all | bytes 5308416 | tf_op jit(solution)/shard_map/all_to_all | solution.py:81
  259.8 2.8 collective-permute-start.34
  263.2 10.2 %all_to_all.21 = f32[8,1,128]{2,1,0:T(1,128)S(1)} all-to-all(f32[8,1,128]{2,1,0:T(1,128)S(1)} %bitcast.31), channel_id=1, replica_groups=mesh['yl'=2,'z'=4,'c'=2,'yh'=2,'x'=4] {'yh','x'}, dimensions={0} | all-to-all | bytes 8192 | tf_op jit(solution)/shard_map/all_to_all | solution.py:113
  278.2 7.4 %select_convert_fusion = (f32[1152,1152]{1,0:T(8,128)}, f32[1152,1152]{1,0:T(8,128)}) fusion(bf16[1152,1152]{1,0:T(8,128)(2,1)} %collective-permute-done.34, pred[]{:T(512)S(6)} %eq.37, bf16[16,72,1152]{2,1,0:T(8,128)(2,1)} %all_to_all.20), kind=kLoop, calls=%fused_computation.15 | loop fusion | flops 5308416 | bytes 15925249 | tf_op jit(solution)/shard_map/convert_element_type | solution.py:127
  (139 shorter events, 48.2 us)
Async XLA Ops:
  0.6 15.5 %copy-start = (bf16[1152,1152]{1,0:T(8,128)(2,1)S(1)}, bf16[1152,1152]{1,0:T(8,128)(2,1)}, u32[]{:S(2)}) copy-start(bf16[1152,1152]{1,0:T(8,128)(2,1)} %param.8) | copy-start | bytes 7962628
  3.1 12.4 %copy-start.5 = (bf16[128,1152]{1,0:T(8,128)(2,1)S(1)}, bf16[128,1152]{1,0:T(8,128)(2,1)}, u32[]{:S(2)}) copy-start(bf16[128,1152]{1,0:T(8,128)(2,1)} %param.6) | copy-start | bytes 884740
  4.3 11.6 %copy-start.12 = (bf16[128,1152]{1,0:T(8,128)(2,1)}, bf16[128,1152]{1,0:T(8,128)(2,1)S(1)}, u32[]{:S(2)}) copy-start(bf16[128,1152]{1,0:T(8,128)(2,1)S(1)} %fusion.15) | copy-start | bytes 884740
  8.3 16.4 %collective-permute-start.7 = (bf16[128,1152]{1,0:T(8,128)(2,1)S(1)}, bf16[128,1152]{1,0:T(8,128)(2,1)S(1)}, u32[]{:S(2)}, u32[]{:S(2)}) collective-permute-start(bf16[128,1152]{1,0:T(8,128)(2,1)S(1)} %get-tuple-element.10), channel_id=1, source_target_pairs={{0,48},{16,0},{32,16},{48,32},{1,49},{17,1},{33,17},{49,33},{2,50}... | collective-permute-start | bytes 884744 | tf_op jit(solution)/shard_map/ppermute | solution.py:41
  12.9 12.8 %collective-permute-start.8 = (bf16[128,1152]{1,0:T(8,128)(2,1)S(1)}, bf16[128,1152]{1,0:T(8,128)(2,1)S(1)}, u32[]{:S(2)}, u32[]{:S(2)}) collective-permute-start(bf16[128,1152]{1,0:T(8,128)(2,1)S(1)} %get-tuple-element.10), channel_id=1, source_target_pairs={{0,16},{16,32},{32,48},{48,0},{1,17},{17,33},{33,49},{49,1},{2,18}... | collective-permute-start | bytes 884744 | tf_op jit(solution)/shard_map/ppermute | solution.py:41
  12.9 13.8 %collective-permute-start.9 = (bf16[128,1152]{1,0:T(8,128)(2,1)S(1)}, bf16[128,1152]{1,0:T(8,128)(2,1)S(1)}, u32[]{:S(2)}, u32[]{:S(2)}) collective-permute-start(bf16[128,1152]{1,0:T(8,128)(2,1)S(1)} %get-tuple-element.10), channel_id=1, source_target_pairs={{0,32},{16,48},{32,0},{48,16},{1,33},{17,49},{33,1},{49,17},{2,34}... | collective-permute-start | bytes 884744 | tf_op jit(solution)/shard_map/ppermute | solution.py:41
  14.2 7.0 %collective-permute-start.10 = (bf16[128,1152]{1,0:T(8,128)(2,1)S(1)}, bf16[128,1152]{1,0:T(8,128)(2,1)S(1)}, u32[]{:S(2)}, u32[]{:S(2)}) collective-permute-start(bf16[128,1152]{1,0:T(8,128)(2,1)S(1)} %get-tuple-element.10), channel_id=1, source_target_pairs={{0,64},{64,0},{1,65},{65,1},{2,66},{66,2},{3,67},{67,3},{4,68},{68... | collective-permute-start | bytes 884744 | tf_op jit(solution)/shard_map/ppermute | solution.py:49
  15.9 9.8 %copy-start.19 = (f32[128]{0:T(128)}, f32[128]{0:T(128)S(1)}, u32[]{:S(2)}) copy-start(f32[128]{0:T(128)S(1)} %add_rsqrt_fusion.3) | copy-start | bytes 1540
  16.1 10.4 %copy-start.14 = (bf16[128,1152]{1,0:T(8,128)(2,1)}, bf16[128,1152]{1,0:T(8,128)(2,1)S(1)}, u32[]{:S(2)}) copy-start(bf16[128,1152]{1,0:T(8,128)(2,1)S(1)} %fusion.10) | copy-start | bytes 884740
  16.8 27.2 %copy-start.3 = (f32[128,1152]{1,0:T(8,128)}, f32[128,1152]{1,0:T(8,128)S(1)}, u32[]{:S(2)}) copy-start(f32[128,1152]{1,0:T(8,128)S(1)} %get-tuple-element.54) | copy-start | bytes 1769476
  17.5 26.5 %copy-start.23 = (f32[128]{0:T(128)}, f32[128]{0:T(128)S(1)}, u32[]{:S(2)}) copy-start(f32[128]{0:T(128)S(1)} %get-tuple-element.52) | copy-start | bytes 1540
  21.2 16.2 %collective-permute-start.11 = (bf16[128,1152]{1,0:T(8,128)(2,1)S(1)}, bf16[128,1152]{1,0:T(8,128)(2,1)S(1)}, u32[]{:S(2)}, u32[]{:S(2)}) collective-permute-start(bf16[128,1152]{1,0:T(8,128)(2,1)S(1)} %collective-permute-done.10), channel_id=1, source_target_pairs={{0,48},{16,0},{32,16},{48,32},{1,49},{17,1},{33,17},{49,33},{2,50}... | collective-permute-start | bytes 884744 | tf_op jit(solution)/shard_map/ppermute | solution.py:41
  22.9 18.1 %collective-permute-start.12 = (bf16[128,1152]{1,0:T(8,128)(2,1)S(1)}, bf16[128,1152]{1,0:T(8,128)(2,1)S(1)}, u32[]{:S(2)}, u32[]{:S(2)}) collective-permute-start(bf16[128,1152]{1,0:T(8,128)(2,1)S(1)} %collective-permute-done.10), channel_id=1, source_target_pairs={{0,16},{16,32},{32,48},{48,0},{1,17},{17,33},{33,49},{49,1},{2,18}... | collective-permute-start | bytes 884744 | tf_op jit(solution)/shard_map/ppermute | solution.py:41
  24.8 16.9 %collective-permute-start.13 = (bf16[128,1152]{1,0:T(8,128)(2,1)S(1)}, bf16[128,1152]{1,0:T(8,128)(2,1)S(1)}, u32[]{:S(2)}, u32[]{:S(2)}) collective-permute-start(bf16[128,1152]{1,0:T(8,128)(2,1)S(1)} %collective-permute-done.10), channel_id=1, source_target_pairs={{0,32},{16,48},{32,0},{48,16},{1,33},{17,49},{33,1},{49,17},{2,34}... | collective-permute-start | bytes 884744 | tf_op jit(solution)/shard_map/ppermute | solution.py:41
  42.4 33.3 %collective-permute-start.14 = (bf16[1024,1152]{1,0:T(8,128)(2,1)}, bf16[1024,1152]{1,0:T(8,128)(2,1)}, u32[]{:S(2)}, u32[]{:S(2)}) collective-permute-start(bf16[1024,1152]{1,0:T(8,128)(2,1)} %get-tuple-element.35), channel_id=1, source_target_pairs={{0,8},{8,0},{1,9},{9,1},{2,10},{10,2},{3,11},{11,3},{4,12},{12,4},... | collective-permute-start | bytes 7077896 | tf_op jit(solution)/shard_map/ppermute | solution.py:49
  45.0 8.9 %collective-permute-start.3 = (bf16[128,1152]{1,0:T(8,128)(2,1)}, bf16[128,1152]{1,0:T(8,128)(2,1)}, u32[]{:S(2)}, u32[]{:S(2)}) collective-permute-start(bf16[128,1152]{1,0:T(8,128)(2,1)} %get-tuple-element.12), channel_id=1, source_target_pairs={{0,4},{4,0},{1,5},{5,1},{2,6},{6,2},{3,7},{7,3},{8,12},{12,8},{9,1... | collective-permute-start | bytes 884744 | tf_op jit(solution)/shard_map/ppermute | solution.py:49
  47.9 8.5 %collective-permute-start = (bf16[128,1152]{1,0:T(8,128)(2,1)}, bf16[128,1152]{1,0:T(8,128)(2,1)}, u32[]{:S(2)}, u32[]{:S(2)}) collective-permute-start(bf16[128,1152]{1,0:T(8,128)(2,1)} %get-tuple-element.12), channel_id=1, source_target_pairs={{0,3},{1,0},{2,1},{3,2},{4,7},{5,4},{6,5},{7,6},{8,11},{9,8},{10,9... | collective-permute-start | bytes 884744 | tf_op jit(solution)/shard_map/ppermute | solution.py:41
  50.4 9.0 %collective-permute-start.1 = (bf16[128,1152]{1,0:T(8,128)(2,1)}, bf16[128,1152]{1,0:T(8,128)(2,1)}, u32[]{:S(2)}, u32[]{:S(2)}) collective-permute-start(bf16[128,1152]{1,0:T(8,128)(2,1)} %get-tuple-element.12), channel_id=1, source_target_pairs={{0,1},{1,2},{2,3},{3,0},{4,5},{5,6},{6,7},{7,4},{8,9},{9,10},{10,1... | collective-permute-start | bytes 884744 | tf_op jit(solution)/shard_map/ppermute | solution.py:41
  50.4 14.0 %collective-permute-start.2 = (bf16[128,1152]{1,0:T(8,128)(2,1)}, bf16[128,1152]{1,0:T(8,128)(2,1)}, u32[]{:S(2)}, u32[]{:S(2)}) collective-permute-start(bf16[128,1152]{1,0:T(8,128)(2,1)} %get-tuple-element.12), channel_id=1, source_target_pairs={{0,2},{1,3},{2,0},{3,1},{4,6},{5,7},{6,4},{7,5},{8,10},{9,11},{10,... | collective-permute-start | bytes 884744 | tf_op jit(solution)/shard_map/ppermute | solution.py:41
  53.9 15.5 %collective-permute-start.4 = (bf16[128,1152]{1,0:T(8,128)(2,1)}, bf16[128,1152]{1,0:T(8,128)(2,1)S(1)}, u32[]{:S(2)}, u32[]{:S(2)}) collective-permute-start(bf16[128,1152]{1,0:T(8,128)(2,1)} %collective-permute-done.3), channel_id=1, source_target_pairs={{0,3},{1,0},{2,1},{3,2},{4,7},{5,4},{6,5},{7,6},{8,11},{9,8},{10,9... | collective-permute-start | bytes 884744 | tf_op jit(solution)/shard_map/ppermute | solution.py:41
  56.4 17.9 %collective-permute-start.5 = (bf16[128,1152]{1,0:T(8,128)(2,1)}, bf16[128,1152]{1,0:T(8,128)(2,1)S(1)}, u32[]{:S(2)}, u32[]{:S(2)}) collective-permute-start(bf16[128,1152]{1,0:T(8,128)(2,1)} %collective-permute-done.3), channel_id=1, source_target_pairs={{0,1},{1,2},{2,3},{3,0},{4,5},{5,6},{6,7},{7,4},{8,9},{9,10},{10,1... | collective-permute-start | bytes 884744 | tf_op jit(solution)/shard_map/ppermute | solution.py:41
  59.4 15.6 %collective-permute-start.6 = (bf16[128,1152]{1,0:T(8,128)(2,1)}, bf16[128,1152]{1,0:T(8,128)(2,1)S(1)}, u32[]{:S(2)}, u32[]{:S(2)}) collective-permute-start(bf16[128,1152]{1,0:T(8,128)(2,1)} %collective-permute-done.3), channel_id=1, source_target_pairs={{0,2},{1,3},{2,0},{3,1},{4,6},{5,7},{6,4},{7,5},{8,10},{9,11},{10,... | collective-permute-start | bytes 884744 | tf_op jit(solution)/shard_map/ppermute | solution.py:41
  99.7 32.9 %collective-permute-start.22 = (bf16[1024,1152]{1,0:T(8,128)(2,1)S(1)}, bf16[1024,1152]{1,0:T(8,128)(2,1)S(1)}, u32[]{:S(2)}, u32[]{:S(2)}) collective-permute-start(bf16[1024,1152]{1,0:T(8,128)(2,1)S(1)} %slice.37), channel_id=1, source_target_pairs={{0,8},{8,0},{1,9},{9,1},{2,10},{10,2},{3,11},{11,3},{4,12},{12,4},... | collective-permute-start | bytes 7077896 | tf_op jit(solution)/shard_map/ppermute | solution.py:49
  111.4 21.2 %copy-start.7 = (bf16[1024,1152]{1,0:T(8,128)(2,1)}, bf16[1024,1152]{1,0:T(8,128)(2,1)S(1)}, u32[]{:S(2)}) copy-start(bf16[1024,1152]{1,0:T(8,128)(2,1)S(1)} %convolution_convert_fusion.1) | copy-start | bytes 7077892
  112.5 8.1 %collective-permute-start.20 = (bf16[128,1152]{1,0:T(8,128)(2,1)S(1)}, bf16[128,1152]{1,0:T(8,128)(2,1)S(1)}, u32[]{:S(2)}, u32[]{:S(2)}) collective-permute-start(bf16[128,1152]{1,0:T(8,128)(2,1)S(1)} %get-tuple-element.24), channel_id=1, source_target_pairs={{0,2},{1,3},{2,0},{3,1},{4,6},{5,7},{6,4},{7,5},{8,10},{9,11},{10,... | collective-permute-start | bytes 884744 | tf_op jit(solution)/shard_map/ppermute | solution.py:45
  112.6 14.5 %collective-permute-start.19 = (bf16[128,1152]{1,0:T(8,128)(2,1)S(1)}, bf16[128,1152]{1,0:T(8,128)(2,1)S(1)}, u32[]{:S(2)}, u32[]{:S(2)}) collective-permute-start(bf16[128,1152]{1,0:T(8,128)(2,1)S(1)} %get-tuple-element.25), channel_id=1, source_target_pairs={{0,3},{1,0},{2,1},{3,2},{4,7},{5,4},{6,5},{7,6},{8,11},{9,8},{10,9... | collective-permute-start | bytes 884744 | tf_op jit(solution)/shard_map/ppermute | solution.py:45
  113.3 18.3 %collective-permute-start.18 = (bf16[128,1152]{1,0:T(8,128)(2,1)S(1)}, bf16[128,1152]{1,0:T(8,128)(2,1)S(1)}, u32[]{:S(2)}, u32[]{:S(2)}) collective-permute-start(bf16[128,1152]{1,0:T(8,128)(2,1)S(1)} %get-tuple-element.26), channel_id=1, source_target_pairs={{0,1},{1,2},{2,3},{3,0},{4,5},{5,6},{6,7},{7,4},{8,9},{9,10},{10,1... | collective-permute-start | bytes 884744 | tf_op jit(solution)/shard_map/ppermute | solution.py:45
  114.1 21.7 %collective-permute-start.17 = (bf16[128,1152]{1,0:T(8,128)(2,1)S(1)}, bf16[128,1152]{1,0:T(8,128)(2,1)}, u32[]{:S(2)}, u32[]{:S(2)}) collective-permute-start(bf16[128,1152]{1,0:T(8,128)(2,1)S(1)} %get-tuple-element.27), channel_id=1, source_target_pairs={{0,2},{1,3},{2,0},{3,1},{4,6},{5,7},{6,4},{7,5},{8,10},{9,11},{10,... | collective-permute-start | bytes 884744 | tf_op jit(solution)/shard_map/ppermute | solution.py:45
  120.6 18.0 %collective-permute-start.16 = (bf16[128,1152]{1,0:T(8,128)(2,1)S(1)}, bf16[128,1152]{1,0:T(8,128)(2,1)}, u32[]{:S(2)}, u32[]{:S(2)}) collective-permute-start(bf16[128,1152]{1,0:T(8,128)(2,1)S(1)} %get-tuple-element.28), channel_id=1, source_target_pairs={{0,3},{1,0},{2,1},{3,2},{4,7},{5,4},{6,5},{7,6},{8,11},{9,8},{10,9... | collective-permute-start | bytes 884744 | tf_op jit(solution)/shard_map/ppermute | solution.py:45
  127.1 13.7 %collective-permute-start.15 = (bf16[128,1152]{1,0:T(8,128)(2,1)}, bf16[128,1152]{1,0:T(8,128)(2,1)}, u32[]{:S(2)}, u32[]{:S(2)}) collective-permute-start(bf16[128,1152]{1,0:T(8,128)(2,1)} %get-tuple-element.23), channel_id=1, source_target_pairs={{0,1},{1,2},{2,3},{3,0},{4,5},{5,6},{6,7},{7,4},{8,9},{9,10},{10,1... | collective-permute-start | bytes 884744 | tf_op jit(solution)/shard_map/ppermute | solution.py:45
  132.5 9.8 %collective-permute-start.21 = (bf16[128,1152]{1,0:T(8,128)(2,1)}, bf16[128,1152]{1,0:T(8,128)(2,1)}, u32[]{:S(2)}, u32[]{:S(2)}) collective-permute-start(bf16[128,1152]{1,0:T(8,128)(2,1)} %add_convert_fusion.1), channel_id=1, source_target_pairs={{0,4},{4,0},{1,5},{5,1},{2,6},{6,2},{3,7},{7,3},{8,12},{12,8},{9,1... | collective-permute-start | bytes 884744 | tf_op jit(solution)/shard_map/ppermute | solution.py:49
  135.8 9.5 %collective-permute-start.28 = (bf16[128,1152]{1,0:T(8,128)(2,1)}, bf16[128,1152]{1,0:T(8,128)(2,1)}, u32[]{:S(2)}, u32[]{:S(2)}) collective-permute-start(bf16[128,1152]{1,0:T(8,128)(2,1)} %get-tuple-element.18), channel_id=1, source_target_pairs={{0,32},{16,48},{32,0},{48,16},{1,33},{17,49},{33,1},{49,17},{2,34}... | collective-permute-start | bytes 884744 | tf_op jit(solution)/shard_map/ppermute | solution.py:45
  135.8 14.2 %collective-permute-start.27 = (bf16[128,1152]{1,0:T(8,128)(2,1)}, bf16[128,1152]{1,0:T(8,128)(2,1)}, u32[]{:S(2)}, u32[]{:S(2)}) collective-permute-start(bf16[128,1152]{1,0:T(8,128)(2,1)} %get-tuple-element.19), channel_id=1, source_target_pairs={{0,48},{16,0},{32,16},{48,32},{1,49},{17,1},{33,17},{49,33},{2,50}... | collective-permute-start | bytes 884744 | tf_op jit(solution)/shard_map/ppermute | solution.py:45
  138.6 15.2 %collective-permute-start.26 = (bf16[128,1152]{1,0:T(8,128)(2,1)}, bf16[128,1152]{1,0:T(8,128)(2,1)}, u32[]{:S(2)}, u32[]{:S(2)}) collective-permute-start(bf16[128,1152]{1,0:T(8,128)(2,1)} %get-tuple-element.20), channel_id=1, source_target_pairs={{0,16},{16,32},{32,48},{48,0},{1,17},{17,33},{33,49},{49,1},{2,18}... | collective-permute-start | bytes 884744 | tf_op jit(solution)/shard_map/ppermute | solution.py:45
  138.6 18.2 %copy-start.4 = (f32[128,1152]{1,0:T(8,128)S(1)}, f32[128,1152]{1,0:T(8,128)}, u32[]{:S(2)}) copy-start(f32[128,1152]{1,0:T(8,128)} %copy-done.3) | copy-start | bytes 1769476
  144.1 14.4 %collective-permute-start.25 = (bf16[128,1152]{1,0:T(8,128)(2,1)}, bf16[128,1152]{1,0:T(8,128)(2,1)S(1)}, u32[]{:S(2)}, u32[]{:S(2)}) collective-permute-start(bf16[128,1152]{1,0:T(8,128)(2,1)} %get-tuple-element.21), channel_id=1, source_target_pairs={{0,32},{16,48},{32,0},{48,16},{1,33},{17,49},{33,1},{49,17},{2,34}... | collective-permute-start | bytes 884744 | tf_op jit(solution)/shard_map/ppermute | solution.py:45
  144.2 18.4 %collective-permute-start.24 = (bf16[128,1152]{1,0:T(8,128)(2,1)}, bf16[128,1152]{1,0:T(8,128)(2,1)S(1)}, u32[]{:S(2)}, u32[]{:S(2)}) collective-permute-start(bf16[128,1152]{1,0:T(8,128)(2,1)} %get-tuple-element.22), channel_id=1, source_target_pairs={{0,48},{16,0},{32,16},{48,32},{1,49},{17,1},{33,17},{49,33},{2,50}... | collective-permute-start | bytes 884744 | tf_op jit(solution)/shard_map/ppermute | solution.py:45
  145.3 21.2 %copy-start.22 = (f32[128]{0:T(128)S(1)}, f32[128]{0:T(128)}, u32[]{:S(2)}) copy-start(f32[128]{0:T(128)} %copy-done.21) | copy-start | bytes 1540
  145.3 21.2 %copy-start.24 = (f32[128]{0:T(128)S(1)}, f32[128]{0:T(128)}, u32[]{:S(2)}) copy-start(f32[128]{0:T(128)} %get-tuple-element.49) | copy-start | bytes 1540
  145.3 20.0 %collective-permute-start.23 = (bf16[128,1152]{1,0:T(8,128)(2,1)}, bf16[128,1152]{1,0:T(8,128)(2,1)S(1)}, u32[]{:S(2)}, u32[]{:S(2)}) collective-permute-start(bf16[128,1152]{1,0:T(8,128)(2,1)} %get-tuple-element.17), channel_id=1, source_target_pairs={{0,16},{16,32},{32,48},{48,0},{1,17},{17,33},{33,49},{49,1},{2,18}... | collective-permute-start | bytes 884744 | tf_op jit(solution)/shard_map/ppermute | solution.py:45
  155.2 10.1 %collective-permute-start.29 = (bf16[128,1152]{1,0:T(8,128)(2,1)S(1)}, bf16[128,1152]{1,0:T(8,128)(2,1)S(1)}, u32[]{:S(2)}, u32[]{:S(2)}) collective-permute-start(bf16[128,1152]{1,0:T(8,128)(2,1)S(1)} %add_convert_fusion), channel_id=1, source_target_pairs={{0,64},{64,0},{1,65},{65,1},{2,66},{66,2},{3,67},{67,3},{4,68},{68... | collective-permute-start | bytes 884744 | tf_op jit(solution)/shard_map/ppermute | solution.py:49
  168.5 3.2 %collective-permute-start.30 = (bf16[256,1152]{1,0:T(8,128)(2,1)S(1)}, bf16[256,1152]{1,0:T(8,128)(2,1)S(1)}, u32[]{:S(2)}, u32[]{:S(2)}) collective-permute-start(bf16[256,1152]{1,0:T(8,128)(2,1)S(1)} %get-tuple-element.30), channel_id=1, source_target_pairs={{0,8},{8,0},{1,9},{9,1},{2,10},{10,2},{3,11},{11,3},{4,12},{12,4},... | collective-permute-start | bytes 1769480 | tf_op jit(solution)/shard_map/ppermute | solution.py:49
  212.2 5.8 %collective-permute-start.33 = (bf16[72,1152]{1,0:T(8,128)(2,1)S(1)}, bf16[72,1152]{1,0:T(8,128)(2,1)S(1)}, u32[]{:S(2)}, u32[]{:S(2)}) collective-permute-start(bf16[72,1152]{1,0:T(8,128)(2,1)S(1)} %reduce_sum.152), channel_id=1, source_target_pairs={{0,4},{64,68},{4,0},{68,64},{1,5},{65,69},{5,1},{69,65},{2,6},{66,... | collective-permute-start | bytes 497672 | tf_op jit(solution)/shard_map/ppermute | solution.py:79
  214.6 6.4 %collective-permute-start.32 = (bf16[72,1152]{1,0:T(8,128)(2,1)S(1)}, bf16[72,1152]{1,0:T(8,128)(2,1)S(1)}, u32[]{:S(2)}, u32[]{:S(2)}) collective-permute-start(bf16[72,1152]{1,0:T(8,128)(2,1)S(1)} %reduce_sum.152), channel_id=1, source_target_pairs={{0,68},{64,0},{4,64},{68,4},{1,69},{65,1},{5,65},{69,5},{2,70},{66... | collective-permute-start | bytes 497672 | tf_op jit(solution)/shard_map/ppermute | solution.py:79
  215.8 7.2 %collective-permute-start.31 = (bf16[72,1152]{1,0:T(8,128)(2,1)S(1)}, bf16[72,1152]{1,0:T(8,128)(2,1)S(1)}, u32[]{:S(2)}, u32[]{:S(2)}) collective-permute-start(bf16[72,1152]{1,0:T(8,128)(2,1)S(1)} %reduce_sum.152), channel_id=1, source_target_pairs={{0,64},{64,4},{4,68},{68,0},{1,65},{65,5},{5,69},{69,1},{2,66},{66... | collective-permute-start | bytes 497672 | tf_op jit(solution)/shard_map/ppermute | solution.py:79
  223.3 50.7 %copy-start.9 = (bf16[128,1152]{1,0:T(8,128)(2,1)S(1)}, bf16[128,1152]{1,0:T(8,128)(2,1)}, u32[]{:S(2)}) copy-start(bf16[128,1152]{1,0:T(8,128)(2,1)} %copy-done.8) | copy-start | bytes 884740
  223.3 50.6 %copy-start.20 = (f32[128]{0:T(128)S(1)}, f32[128]{0:T(128)}, u32[]{:S(2)}) copy-start(f32[128]{0:T(128)} %copy-done.19) | copy-start | bytes 1540
  259.8 18.4 %collective-permute-start.34 = (bf16[1152,1152]{1,0:T(8,128)(2,1)}, bf16[1152,1152]{1,0:T(8,128)(2,1)}, u32[]{:S(2)}, u32[]{:S(2)}) collective-permute-start(bf16[1152,1152]{1,0:T(8,128)(2,1)} %bitcast.7), channel_id=1, source_target_pairs={{0,8},{8,0},{1,9},{9,1},{2,10},{10,2},{3,11},{11,3},{4,12},{12,4},... | collective-permute-start | bytes 7962632 | tf_op jit(solution)/shard_map/ppermute | solution.py:49
  (12 other events, 57.2 us)

commit v2 on v1

--- a/solution.py
+++ b/solution.py
@@ -1,6 +1,10 @@
+import functools
+
 import jax
 import jax.numpy as jnp
 from jax import lax
+from jax.experimental import pallas as pl
+from jax.experimental.pallas import tpu as pltpu
 from jax.sharding import Mesh, PartitionSpec as P
 
 EPS = 1e-06
@@ -49,25 +53,211 @@
     return lax.ppermute(block, axis, [(0, 1), (1, 0)])
 
 
-STEPS = (1, 3, 2)
-
-
-def gather8(block, ring, pair):
-    other = swap(block, pair)
-    near = [block] + [fetch(block, ring, s) for s in STEPS]
-    far = [other] + [fetch(other, ring, s) for s in STEPS]
-    return near + far
-
-
-def scatter8(parts, ring, pair):
-    def ring_sum(four):
-        total = four[0].astype(F32)
-        for s, part in zip(STEPS, four[1:]):
-            total = total + give(part, ring, s).astype(F32)
-        return total
-
-    far = swap(ring_sum(parts[4:]).astype(BF), pair)
-    return ring_sum(parts[:4]) + far.astype(F32)
+STEPS = (2, 1, 3)
+
+
+def ring_fetch(block, ring):
+    return [block] + [fetch(block, ring, s) for s in STEPS]
+
+
+LOG2E = 1.4426950408889634
+VMEM = pl.BlockSpec(memory_space=pltpu.VMEM)
+SMEM = pl.BlockSpec(memory_space=pltpu.SMEM)
+HBM = pl.BlockSpec(memory_space=pltpu.HBM)
+TILE = 512
+WIDE = 384
+LANES = 128
+
+
+def params(mib):
+    return pltpu.CompilerParams(vmem_limit_bytes=mib * 2**20)
+
+
+def cost(flops, mib):
+    return pl.CostEstimate(flops=flops, bytes_accessed=mib * 2**20, transcendentals=0)
+
+
+def in_hbm(value):
+    return pltpu.with_memory_space_constraint(value, pltpu.HBM)
+
+
+def load_all(pairs, sems):
+    copies = [pltpu.make_async_copy(ref, into, sems.at[at]) for at, (ref, into) in enumerate(pairs)]
+    for copy in copies:
+        copy.start()
+    for copy in copies:
+        copy.wait()
+
+
+def cell(scores, temper, offset):
+    e = jnp.exp2(scores * (temper * LOG2E) + offset * LOG2E)
+    u = 1.0 + e
+    small = e * (LOG2E - e * (0.5 * LOG2E - e * (LOG2E / 3)))
+    return temper * e / u, jnp.where(e < 0.01, small, jnp.log2(u))
+
+
+def positive(scores, temper, offset):
+    q, loss = cell(-scores, temper, -offset)
+    return -q, loss
+
+
+def pair_kernel(n_img, rows, *refs):
+    img_refs = refs[:n_img]
+    txt_refs = refs[n_img : n_img + 2]
+    place_ref, temper_ref, offset_ref = refs[n_img + 2 : n_img + 5]
+    q_ref, loss_ref, images, texts, out_ref, even, odd, sems = refs[n_img + 5 :]
+    n_txt = texts.shape[0] // rows
+    moves = [(ref, images.at[pl.ds(at * rows, rows)]) for at, ref in enumerate(img_refs)]
+    for at in range(n_txt):
+        start = pl.multiple_of(place_ref[at % (n_txt // 2)] * rows, rows)
+        txt_ref = txt_refs[at // (n_txt // 2)]
+        moves.append((txt_ref.at[pl.ds(start, rows)], texts.at[pl.ds(at * rows, rows)]))
+    load_all(moves, sems)
+    temper, offset = temper_ref[0], offset_ref[0]
+    tiles = texts.shape[0] // TILE
+    loss_ref[...] = jnp.zeros_like(loss_ref)
+
+    def columns(tile):
+        return pl.ds(pl.multiple_of(tile * TILE, TILE), TILE)
+
+    def multiply(tile, out):
+        out[...] = lax.dot_general(
+            images[...], texts[columns(tile), :], (((1,), (1,)), ((), ())), preferred_element_type=F32
+        )
+
+    def finish(tile, scores):
+        q, loss = cell(scores[...], temper, offset)
+        q_ref[:, columns(tile)] = q.astype(BF)
+        loss_ref[...] += sum(loss[:, at : at + LANES] for at in range(0, TILE, LANES))
+
+    multiply(0, even)
+    own = even[:rows, :rows]
+    here = lax.broadcasted_iota(jnp.int32, (rows, rows), 0) == lax.broadcasted_iota(jnp.int32, (rows, rows), 1)
+    plain_q, plain_loss = cell(own, temper, offset)
+    own_q, own_loss = positive(own, temper, offset)
+    own_q = jnp.where(here, own_q, plain_q).astype(BF)
+    own_loss = jnp.where(here, own_loss - plain_loss, 0.0)
+
+    def body(pair, carry):
+        multiply(2 * pair + 1, odd)
+        finish(2 * pair, even)
+        multiply(jnp.minimum(2 * pair + 2, tiles - 1), even)
+        finish(2 * pair + 1, odd)
+        return carry
+
+    lax.fori_loop(0, tiles // 2, body, 0)
+    q_ref[:rows, :rows] = own_q
+    loss_ref[:rows, :] += own_loss
+    half = texts.shape[0] // 2
+    for at in range(0, images.shape[1], WIDE):
+        out_ref[:, at : at + WIDE] = lax.dot_general(
+            q_ref[:, half:], images[:, at : at + WIDE], (((0,), (0,)), ((), ())), preferred_element_type=F32
+        ).astype(BF)
+
+
+def pair_call(images, texts, place, temper, offset):
+    rows, width = images[0].shape
+    m, n = len(images) * rows, 2 * texts[0].shape[0]
+    return pl.pallas_call(
+        functools.partial(pair_kernel, len(images), rows),
+        in_specs=[HBM] * (len(images) + 2) + [SMEM] * 3,
+        out_specs=[VMEM] * 5,
+        out_shape=[
+            pltpu.VMEM((m, n), BF),
+            pltpu.VMEM((m, LANES), F32),
+            pltpu.VMEM((m, width), BF),
+            pltpu.VMEM((n, width), BF),
+            pltpu.HBM((n // 2, width), BF),
+        ],
+        scratch_shapes=[pltpu.VMEM((m, TILE), F32)] * 2 + [pltpu.SemaphoreType.DMA((len(images) + n // rows,))],
+        compiler_params=params(32),
+        cost_estimate=cost(4 * m * n * width, 10),
+        name="pair",
+    )(*[in_hbm(block) for block in (*images, *texts)], place, temper, offset)
+
+
+def cut_blocks(product, at, rows, out_refs, own_ref):
+    columns = slice(at, at + product.shape[1])
+    for place, ref in enumerate((own_ref, *out_refs)):
+        for side, first in enumerate((4 * rows, 0)):
+            block = product[first + place * rows : first + (place + 1) * rows]
+            ref[side * rows : (side + 1) * rows, columns] = block.astype(ref.dtype)
+
+
+def grad_img_kernel(rows, q_ref, texts, loss_ref, *refs):
+    width = texts.shape[1]
+    for at in range(0, width, WIDE):
+        product = jnp.dot(q_ref[...], texts[:, at : at + WIDE], preferred_element_type=F32)
+        cut_blocks(product, at, rows, refs[:3], refs[3])
+    cut_blocks(loss_ref[...], width, rows, refs[:3], refs[3])
+
+
+def grad_txt_kernel(rows, q_ref, images, got_ref, place_ref, out_ref, got, total, sems):
+    load_all([(got_ref, got)], sems)
+    width = images.shape[1]
+    for at in range(0, width, WIDE):
+        product = lax.dot_general(
+            q_ref[:, : got.shape[0]], images[:, at : at + WIDE], (((0,), (0,)), ((), ())), preferred_element_type=F32
+        )
+        total[:, at : at + WIDE] = (product + got[:, at : at + WIDE].astype(F32)).astype(BF)
+    blocks = got.shape[0] // rows
+    moves = []
+    for at in range(blocks):
+        start = pl.multiple_of(place_ref[at] * rows, rows)
+        moves.append((total.at[pl.ds(at * rows, rows)], out_ref.at[pl.ds(start, rows)]))
+    load_all(moves, sems)
+
+
+def cut_shapes(rows, width):
+    return [pltpu.HBM((2 * rows, width), BF)] * 3 + [pltpu.HBM((2 * rows, width), F32)]
+
+
+def grad_img_call(q, texts, loss, rows):
+    width = texts.shape[1] + LANES
+    return pl.pallas_call(
+        functools.partial(grad_img_kernel, rows),
+        in_specs=[VMEM] * 3,
+        out_specs=[VMEM] * 4,
+        out_shape=cut_shapes(rows, width),
+        compiler_params=params(24),
+        cost_estimate=cost(2 * q.shape[0] * q.shape[1] * width, 4),
+        name="grad_img",
+    )(q, texts, loss)
+
+
+def grad_txt_call(q, images, got, place, rows):
+    width = images.shape[1]
+    return pl.pallas_call(
+        functools.partial(grad_txt_kernel, rows),
+        in_specs=[VMEM, VMEM, HBM, SMEM],
+        out_specs=HBM,
+        out_shape=pltpu.HBM(got.shape, BF),
+        scratch_shapes=[pltpu.VMEM(got.shape, BF)] * 2 + [pltpu.SemaphoreType.DMA((got.shape[0] // rows,))],
+        compiler_params=params(24),
+        cost_estimate=cost(2 * got.shape[0] * q.shape[0] * width, 6),
+        name="grad_txt",
+    )(q, images, in_hbm(got), place)
+
+
+def ring_give(parts, ring):
+    return [give(part, ring, s) for s, part in zip(STEPS, parts)] + [parts[3]]
+
+
+def pair_sum(parts, pair):
+    rows = parts[0].shape[0] // 2
+    total = sum(part.astype(F32) for part in parts)
+    return total[rows:], swap(total[:rows].astype(BF), pair)
+
+
+def text_places():
+    yl, z = lax.axis_index("yl"), lax.axis_index("z")
+    places = [(yl ^ other) * 4 + (z + s) % 4 for other in (0, 1) for s in (0,) + STEPS]
+    return jnp.stack(places).astype(jnp.int32)
+
+
+def gather_text(block):
+    spread = jnp.broadcast_to(block[None], (8,) + block.shape)
+    return lax.all_to_all(spread, ("yl", "z"), 0, 0, tiled=True).reshape(8 * block.shape[0], block.shape[1])
 
 
 def reduce_weights(part):
@@ -90,28 +280,26 @@
 def per_device(image_feats, text_feats, image_weight, text_weight, temper, offset):
     rows = image_feats.shape[0]
     core = lax.axis_index("c")
+    text_state = tower(text_feats, text_weight)
     image_state = tower(image_feats, image_weight)
-    text_state = tower(text_feats, text_weight)
-    images = jnp.concatenate(gather8(image_state[5], "x", "yh"))
-    texts_same = jnp.concatenate(gather8(text_state[5], "z", "yl"))
-    texts = jnp.concatenate([texts_same, swap(texts_same, "c")])
-    scores = lax.dot_general(images, texts, (((1,), (1,)), ((), ())), preferred_element_type=F32)
-    logits = temper[0] * scores + offset[0]
-    near = lax.broadcasted_iota(jnp.int32, logits.shape, 0)
-    signs = jnp.where(
-        (near == lax.broadcasted_iota(jnp.int32, logits.shape, 1)) & (near < rows), 1.0, -1.0
-    ).astype(F32)
-    flipped = -signs * logits
-    loss_rows = jnp.sum(jax.nn.softplus(flipped), 1)
-    weights = (-temper[0] * signs * jax.nn.sigmoid(flipped)).astype(BF)
-    grad_img = jnp.dot(weights, texts, preferred_element_type=F32).astype(BF)
-    grad_txt = lax.dot_general(weights, images, (((0,), (0,)), ((), ())), preferred_element_type=F32)
-    half = grad_txt.shape[0] // 2
-    grad_txt = (grad_txt[:half] + swap(grad_txt[half:].astype(BF), "c").astype(F32)).astype(BF)
-    grad_img = scatter8(jnp.split(grad_img, 8), "x", "yh")
-    grad_txt = scatter8(jnp.split(grad_txt, 8), "z", "yl")
-    loss8 = lax.all_to_all(loss_rows.reshape(8, rows)[reorder()], ("yh", "x"), 0, 0, tiled=True)
-    image_loss = jnp.sum(loss8, 0)
+    img, txt = image_state[5], text_state[5]
+    far_img, txt = lax.optimization_barrier((swap(img, "yh"), txt))
+    texts = gather_text(txt)
+    images = ring_fetch(img, "x") + ring_fetch(far_img, "x")
+    texts, images = lax.optimization_barrier((texts, images))
+    texts = [texts, swap(texts, "c")]
+    place = text_places()
+    q, loss, images, texts, sent = pair_call(images, texts, place, temper, offset)
+    got = swap(sent, "c")
+    img_parts = ring_give(grad_img_call(q, texts, loss, rows), "x")
+    txt_parts = grad_txt_call(q, images, got, place, rows).reshape(8, rows, -1)
+    img_parts, _ = lax.optimization_barrier((img_parts, txt_parts))
+    txt_parts = lax.all_to_all(txt_parts, ("yl", "z"), 0, 0, tiled=True)
+    img_near, img_far = pair_sum(img_parts, "yh")
+    grad_img = img_near + img_far.astype(F32)
+    grad_txt = jnp.sum(txt_parts.astype(F32), 0)
+    image_loss = jnp.sum(grad_img[:, img.shape[1] :], 1) * (1.0 / LOG2E)
+    grad_img = grad_img[:, : img.shape[1]]
     image_gp = back_proj(image_state, grad_img).astype(BF)
     text_gp = back_proj(text_state, grad_txt).astype(BF)
     image_pack = jnp.concatenate([image_state[2], image_gp])
@@ -130,14 +318,6 @@
     return (image_loss, grad_image, grad_text, grad_image_weight, grad_text_weight)
 
 
-def reorder():
-    yh, x = lax.axis_index("yh"), lax.axis_index("x")
-    owner = jnp.arange(8)
-    step = (owner % 4 - x) % 4
-    place = jnp.where(step == 2, 3, jnp.where(step == 3, 2, step))
-    return (owner // 4 != yh).astype(jnp.int32) * 4 + place
-
-
 def solution(mesh):
     rows = P(AXES, None)
     in_specs = (rows, rows, P(), P(), P(), P())

time: 286 us -> 253 us (0.88)
  Pallas kernels: 0 us -> 33.2 us
  matrix products: 32.3 us -> 4.45 us
  local copies, waits for them, and re-layouts: 23.2 us -> 7.79 us
  blocking collectives: 84 us -> 73.4 us
  starting transfers between devices: 49.8 us -> 41.2 us
    pallas_call x0 -> x3, Pallas kernels: none -> 33.2 us  [the longest x1 17.8 us: pair_call(): pl.pallas_call(functools.partial(pair_kernel, len(images), rows), in_spec...]
    dot_general x3 -> x0, matrix products: 26 us -> none  [the longest x1 14.4 us: per_device(): lax.dot_general(images, texts, (((1,), (1,)), ((), ())), preferred_elemen...]
    ppermute x12 -> x3, waiting for transfers between devices: 30.8 us -> 15.2 us  [give(): return lax.ppermute(block, axis, [(i, (i + step) % 4) for i in range(4)])]
    ppermute x8 -> x6, waiting for transfers between devices: 7.16 us -> 21.7 us  [swap(): return lax.ppermute(block, axis, [(0, 1), (1, 0)])]
    all_to_all x0 -> x2, starting transfers between devices: none -> 10.4 us  [the longest x1 6.06 us: gather_text(): lax.all_to_all(spread, ('yl', 'z'), 0, 0, tiled=True)]
    all_to_all x1 -> x0, blocking collectives: 10.2 us -> none  [per_device(): lax.all_to_all(loss_rows.reshape(8, rows)[reorder()], ('yh', 'x'), 0, 0,...]
    unnamed x63 -> x50, local copies, waits for them, and re-layouts: 14.9 us -> 4.96 us
    ppermute x12 -> x6, starting transfers between devices: 18 us -> 8.5 us  [fetch(): return lax.ppermute(block, axis, [(i, (i - step) % 4) for i in range(4)])]
  transfers between devices with their start and end apart: 35 -> 20, of which waited for: 24 -> 14; matrix products, arithmetic and copies ran while one was open for 13% -> 5% of each run, Pallas kernels for 0% -> 6%
where the time goes in v2:
time: 253 us; the launch traced here: 252 us
  blocking collectives  73.4 us (29%)
  waiting for transfers between devices  63.8 us (25%)
  starting transfers between devices  41.2 us (16%)
  Pallas kernels  33.2 us (13%)
  other arithmetic  25.8 us (10%)
  local copies, waits for them, and re-layouts  7.79 us (3%)
  matrix products  4.45 us (2%)
    all_to_all x1, blocking collectives, reduce_weights(): lax.all_to_all(part.astype(BF).reshape(16, rows // 16, cols), ('z', 'x'),...  38.7 us
    all_to_all x1, blocking collectives, reduce_weights(): lax.all_to_all(jnp.broadcast_to(total[None], (16,) + total.shape), ('z',...  34.6 us
    ppermute x6, waiting for transfers between devices, swap(): return lax.ppermute(block, axis, [(0, 1), (1, 0)])  21.7 us
    ppermute x6, waiting for transfers between devices, fetch(): return lax.ppermute(block, axis, [(i, (i - step) % 4) for i in range(4)])  19.7 us
    pallas_call x1, Pallas kernels, pair_call(): pl.pallas_call(functools.partial(pair_kernel, len(images), rows), in_spec...  17.8 us
    ppermute x6, starting transfers between devices, swap(): return lax.ppermute(block, axis, [(0, 1), (1, 0)])  15.4 us
    ppermute x3, waiting for transfers between devices, give(): return lax.ppermute(block, axis, [(i, (i + step) % 4) for i in range(4)])  15.2 us
    ppermute x6, starting transfers between devices, fetch(): return lax.ppermute(block, axis, [(i, (i - step) % 4) for i in range(4)])  8.5 us
  transfers between devices with their start and end apart: 20, of which 14 were waited for; matrix products, arithmetic and copies ran while one was open for 5% of the time, Pallas kernels for 6%

profile of v2, /device:TPU:1, one launch (start us, length us, event | category | flops | bytes accessed | tf_op | source)
XLA Modules:
  0.0 251.9 jit_solution(16603009332614988793)
XLA Ops:
  0.6 1.2 convert_reduce_fusion.2
  1.9 1.2 fusion.17
  3.1 1.2 fusion.4
  5.7 3.8 %collective-permute-start = (bf16[128,1152]{1,0:T(8,128)(2,1)S(1)}, bf16[128,1152]{1,0:T(8,128)(2,1)}, u32[]{:S(2)}, u32[]{:S(2)}) collective-permute-start(bf16[128,1152]{1,0:T(8,128)(2,1)S(1)} %multiply_convert_fusion.1.refs_0_), channel_id=1, source_target_pairs={{0,4},{4,0},{1,5},{5,1},{2,6},{6,2},{3,7},{7,3},{8,12},{12,8},{9,1... | collective-permute-start | bytes 884744 | tf_op jit(solution)/shard_map/ppermute | solution.py:53
  12.6 3.5 %collective-permute-done.refs_4_ = bf16[128,1152]{1,0:T(8,128)(2,1)} collective-permute-done((bf16[128,1152]{1,0:T(8,128)(2,1)S(1)}, bf16[128,1152]{1,0:T(8,128)(2,1)}, u32[]{:S(2)}, u32[]{:S(2)}) %collective-permute-start) | collective-permute-done | bytes 294944 | tf_op jit(solution)/shard_map/ppermute | solution.py:53
  16.1 1.7 broadcast_in_dim.4
  17.8 6.1 %all-to-all-start = ((bf16[8,128,1152]{2,1,0:T(8,128)(2,1)}), bf16[8,128,1152]{2,1,0:T(8,128)(2,1)}, u32[]{:S(2)}, u32[]{:S(2)}) async-start(bf16[8,128,1152]{2,1,0:T(8,128)(2,1)} %broadcast_in_dim.4), calls=%async_computation | async-start | bytes 4718592 | tf_op jit(solution)/shard_map/all_to_all | solution.py:260
  23.8 1.2 collective-permute-start.3
  25.0 1.5 collective-permute-start.2
  26.5 1.5 collective-permute-start.1
  28.3 2.4 collective-permute-start.5
  30.7 1.3 collective-permute-done.3.refs_3_
  32.0 1.6 collective-permute-start.4
  33.6 5.7 %collective-permute-done.1.refs_1_ = bf16[128,1152]{1,0:T(8,128)(2,1)} collective-permute-done((bf16[128,1152]{1,0:T(8,128)(2,1)}, bf16[128,1152]{1,0:T(8,128)(2,1)}, u32[]{:S(2)}, u32[]{:S(2)}) %collective-permute-start.1) | collective-permute-done | bytes 294944 | tf_op jit(solution)/shard_map/ppermute | solution.py:45
  39.4 5.6 %collective-permute-done.6.refs_7_ = bf16[128,1152]{1,0:T(8,128)(2,1)} collective-permute-done((bf16[128,1152]{1,0:T(8,128)(2,1)}, bf16[128,1152]{1,0:T(8,128)(2,1)}, u32[]{:S(2)}, u32[]{:S(2)}) %collective-permute-start.6) | collective-permute-done | bytes 294944 | tf_op jit(solution)/shard_map/ppermute | solution.py:45
  45.0 7.0 %collective-permute-done.4.refs_5_ = bf16[128,1152]{1,0:T(8,128)(2,1)} collective-permute-done((bf16[128,1152]{1,0:T(8,128)(2,1)}, bf16[128,1152]{1,0:T(8,128)(2,1)}, u32[]{:S(2)}, u32[]{:S(2)}) %collective-permute-start.4) | collective-permute-done | bytes 294944 | tf_op jit(solution)/shard_map/ppermute | solution.py:45
  52.9 1.9 collective-permute-start.7
  56.2 3.1 %collective-permute-done.7.refs_9_ = bf16[1024,1152]{1,0:T(8,128)(2,1)} collective-permute-done((bf16[1024,1152]{1,0:T(8,128)(2,1)}, bf16[1024,1152]{1,0:T(8,128)(2,1)}, u32[]{:S(2)}, u32[]{:S(2)}) %collective-permute-start.7) | collective-permute-done | bytes 2359328 | tf_op jit(solution)/shard_map/ppermute | solution.py:53
  59.3 17.8 %pair.1 = (bf16[1024,2048]{1,0:T(8,128)(2,1)S(1)}, f32[1024,128]{1,0:T(8,128)S(1)}, bf16[1024,1152]{1,0:T(8,128)(2,1)S(1)}, bf16[2048,1152]{1,0:T(8,128)(2,1)S(1)}, bf16[1024,1152]{1,0:T(8,128)(2,1)}) custom-call(bf16[128,1152]{1,0:T(8,128)(2,1)} %copy-done.18, bf16[128,1152]{1,0:T(8,128)(2,1)} %collective-permute-done.1.refs_1_, ...), custom_call_target="tpu_custom_call" | custom-call | flops 9663676416 | bytes 10485760 | tf_op jit(solution)/shard_map/pair/pallas_call | solution.py:161
  77.7 8.3 %grad_img.1 = (bf16[256,1280]{1,0:T(8,128)(2,1)}, bf16[256,1280]{1,0:T(8,128)(2,1)}, bf16[256,1280]{1,0:T(8,128)(2,1)}, f32[256,1280]{1,0:T(8,128)}) custom-call(bf16[1024,2048]{1,0:T(8,128)(2,1)S(1)} %get-tuple-element.40.q_ref, bf16[2048,1152]{1,0:T(8,128)(2,1)S(1)} %get-tuple-element.41.texts, f32[1024,128]{1,0:T(8,128)S(1)} %get-tuple-element.42.loss_ref), custom_call_target="tpu_custom_call" | custom-call | flops 5368709120 | bytes 4194304 | tf_op jit(solution)/shard_map/grad_img/pallas_call | solution.py:217
  86.0 1.7 collective-permute-start.8
  88.2 2.2 collective-permute-start.10
  90.4 1.4 copy-done.17
  91.8 7.1 %grad_txt.1 = bf16[1024,1152]{1,0:T(8,128)(2,1)} custom-call(bf16[1024,2048]{1,0:T(8,128)(2,1)S(1)} %get-tuple-element.40.q_ref, bf16[1024,1152]{1,0:T(8,128)(2,1)S(1)} %get-tuple-element.47.images, bf16[1024,1152]{1,0:T(8,128)(2,1)} %copy-done.17, s32[8]{0:T(128)S(1)} %stack.35.refs_10_.place_ref), custom_call_target="tpu_custom_call" | custom-call | flops 2415919104 | bytes 6291456 | tf_op jit(solution)/shard_map/grad_txt/pallas_call | solution.py:230
  98.9 4.4 %all-to-all-start.1 = ((bf16[8,128,1152]{2,1,0:T(8,128)(2,1)}), bf16[8,128,1152]{2,1,0:T(8,128)(2,1)}, u32[]{:S(2)}, u32[]{:S(2)}) async-start(bf16[8,128,1152]{2,1,0:T(8,128)(2,1)} %bitcast.23), calls=%async_computation.1 | async-start | bytes 4718592 | tf_op jit(solution)/shard_map/all_to_all | solution.py:297
  104.0 14.5 %collective-permute-done.9 = bf16[256,1280]{1,0:T(8,128)(2,1)} collective-permute-done((bf16[256,1280]{1,0:T(8,128)(2,1)}, bf16[256,1280]{1,0:T(8,128)(2,1)}, u32[]{:S(2)}, u32[]{:S(2)}) %collective-permute-start.9) | collective-permute-done | bytes 655392 | tf_op jit(solution)/shard_map/ppermute | solution.py:49
  118.5 2.1 add_add_fusion
  120.7 1.0 copy-done.8
  122.5 2.6 %collective-permute-start.12 = (bf16[128,1280]{1,0:T(8,128)(2,1)}, bf16[128,1280]{1,0:T(8,128)(2,1)}, u32[]{:S(2)}, u32[]{:S(2)}) collective-permute-start(bf16[128,1280]{1,0:T(8,128)(2,1)} %slice.46), channel_id=1, source_target_pairs={{0,4},{4,0},{1,5},{5,1},{2,6},{6,2},{3,7},{7,3},{8,12},{12,8},{9,1... | collective-permute-start | bytes 983048 | tf_op jit(solution)/shard_map/ppermute | solution.py:53
  125.1 13.5 %collective-permute-done.12 = bf16[128,1280]{1,0:T(8,128)(2,1)} collective-permute-done((bf16[128,1280]{1,0:T(8,128)(2,1)}, bf16[128,1280]{1,0:T(8,128)(2,1)}, u32[]{:S(2)}, u32[]{:S(2)}) %collective-permute-start.12) | collective-permute-done | bytes 327712 | tf_op jit(solution)/shard_map/ppermute | solution.py:53
  138.6 1.2 slice_add_fusion
  140.7 1.5 subtract_convert_fusion.1
  142.3 2.2 convert_reduce_fusion
  144.4 1.2 multiply_reduce_fusion
  147.4 1.7 collective-permute-start.13
  149.2 1.6 collective-permute-done.13
  151.8 38.7 %all_to_all.20 = bf16[16,72,1152]{2,1,0:T(8,128)(2,1)} all-to-all(bf16[16,72,1152]{2,1,0:T(8,128)(2,1)S(1)} %bitcast.24), channel_id=1, replica_groups=mesh['yl'=2,'z'=4,'c'=2,'yh'=2,'x'=4] {'z','x'}, dimensions={0} | all-to-all | bytes 5308416 | tf_op jit(solution)/shard_map/all_to_all | solution.py:265
  190.5 2.2 reduce_sum.152
  192.7 1.0 collective-permute-start.16
  195.2 1.8 collective-permute-done.16
  197.0 4.0 %collective-permute-done.15 = bf16[72,1152]{1,0:T(8,128)(2,1)S(1)} collective-permute-done((bf16[72,1152]{1,0:T(8,128)(2,1)S(1)}, bf16[72,1152]{1,0:T(8,128)(2,1)S(1)}, u32[]{:S(2)}, u32[]{:S(2)}) %collective-permute-start.15) | collective-permute-done | bytes 165920 | tf_op jit(solution)/shard_map/ppermute | solution.py:269
  201.8 34.6 %all_to_all.21 = bf16[16,72,1152]{2,1,0:T(8,128)(2,1)S(1)} all-to-all(bf16[16,72,1152]{2,1,0:T(8,128)(2,1)S(1)} %broadcast_in_dim.5), channel_id=1, replica_groups=mesh['yl'=2,'z'=4,'c'=2,'yh'=2,'x'=4] {'z','x'}, dimensions={0} | all-to-all | bytes 5308416 | tf_op jit(solution)/shard_map/all_to_all | solution.py:271
  236.4 4.7 %collective-permute-start.17 = (bf16[1152,1152]{1,0:T(8,128)(2,1)S(1)}, bf16[1152,1152]{1,0:T(8,128)(2,1)S(1)}, u32[]{:S(2)}, u32[]{:S(2)}) collective-permute-start(bf16[1152,1152]{1,0:T(8,128)(2,1)S(1)} %bitcast.22), channel_id=1, source_target_pairs={{0,8},{8,0},{1,9},{9,1},{2,10},{10,2},{3,11},{11,3},{4,12},{12,4},... | collective-permute-start | bytes 7962632 | tf_op jit(solution)/shard_map/ppermute | solution.py:53
  242.6 1.0 fusion.26
  243.7 1.1 fusion.16
  244.8 1.0 fusion.25
  245.8 1.1 fusion.12
  246.9 5.0 %select_convert_fusion = (f32[1152,1152]{1,0:T(8,128)}, f32[1152,1152]{1,0:T(8,128)}) fusion(bf16[1152,1152]{1,0:T(8,128)(2,1)S(1)} %collective-permute-done.17, pred[]{:T(512)S(6)} %eq.15, bf16[16,72,1152]{2,1,0:T(8,128)(2,1)S(1)} %all_to_all.21), kind=kLoop, calls=%fused_computation.2 | loop fusion | flops 5308416 | bytes 15925249 | tf_op jit(solution)/shard_map/convert_element_type | solution.py:315
  (89 shorter events, 15.6 us)
Async XLA Ops:
  0.6 3.7 %copy-start = (bf16[1152,1152]{1,0:T(8,128)(2,1)S(1)}, bf16[1152,1152]{1,0:T(8,128)(2,1)}, u32[]{:S(2)}) copy-start(bf16[1152,1152]{1,0:T(8,128)(2,1)} %param.8) | copy-start | bytes 7962628
  1.9 7.6 %copy-start.6 = (bf16[128,1152]{1,0:T(8,128)(2,1)S(1)}, bf16[128,1152]{1,0:T(8,128)(2,1)}, u32[]{:S(2)}) copy-start(bf16[128,1152]{1,0:T(8,128)(2,1)} %param.7) | copy-start | bytes 884740
  4.3 5.6 %copy-start.13 = (bf16[128,1152]{1,0:T(8,128)(2,1)}, bf16[128,1152]{1,0:T(8,128)(2,1)S(1)}, u32[]{:S(2)}) copy-start(bf16[128,1152]{1,0:T(8,128)(2,1)S(1)} %fusion.4) | copy-start | bytes 884740
  4.3 6.4 %copy-start.1 = (bf16[1152,1152]{1,0:T(8,128)(2,1)S(1)}, bf16[1152,1152]{1,0:T(8,128)(2,1)}, u32[]{:S(2)}) copy-start(bf16[1152,1152]{1,0:T(8,128)(2,1)} %param.9) | copy-start | bytes 7962628
  5.6 3.9 %copy-start.21 = (f32[128]{0:T(128)}, f32[128]{0:T(128)S(1)}, u32[]{:S(2)}) copy-start(f32[128]{0:T(128)S(1)} %get-tuple-element.68) | copy-start | bytes 1540
  5.7 6.7 %copy-start.18 = (bf16[128,1152]{1,0:T(8,128)(2,1)}, bf16[128,1152]{1,0:T(8,128)(2,1)S(1)}, u32[]{:S(2)}) copy-start(bf16[128,1152]{1,0:T(8,128)(2,1)S(1)} %multiply_convert_fusion.1.refs_0_) | copy-start | bytes 884740
  5.7 10.4 %collective-permute-start = (bf16[128,1152]{1,0:T(8,128)(2,1)S(1)}, bf16[128,1152]{1,0:T(8,128)(2,1)}, u32[]{:S(2)}, u32[]{:S(2)}) collective-permute-start(bf16[128,1152]{1,0:T(8,128)(2,1)S(1)} %multiply_convert_fusion.1.refs_0_), channel_id=1, source_target_pairs={{0,4},{4,0},{1,5},{5,1},{2,6},{6,2},{3,7},{7,3},{8,12},{12,8},{9,1... | collective-permute-start | bytes 884744 | tf_op jit(solution)/shard_map/ppermute | solution.py:53
  9.9 0.6 copy-start.19
  10.7 1.7 copy-start.15
  11.4 0.8 copy-start.3
  12.0 0.6 copy-start.23
  17.8 35.1 %all-to-all-start = ((bf16[8,128,1152]{2,1,0:T(8,128)(2,1)}), bf16[8,128,1152]{2,1,0:T(8,128)(2,1)}, u32[]{:S(2)}, u32[]{:S(2)}) async-start(bf16[8,128,1152]{2,1,0:T(8,128)(2,1)} %broadcast_in_dim.4), calls=%async_computation | async-start | bytes 4718592 | tf_op jit(solution)/shard_map/all_to_all | solution.py:260
  23.8 8.2 %collective-permute-start.3 = (bf16[128,1152]{1,0:T(8,128)(2,1)}, bf16[128,1152]{1,0:T(8,128)(2,1)}, u32[]{:S(2)}, u32[]{:S(2)}) collective-permute-start(bf16[128,1152]{1,0:T(8,128)(2,1)} %copy-done.18), channel_id=1, source_target_pairs={{0,1},{1,2},{2,3},{3,0},{4,5},{5,6},{6,7},{7,4},{8,9},{9,10},{10,1... | collective-permute-start | bytes 884744 | tf_op jit(solution)/shard_map/ppermute | solution.py:45
  25.0 8.6 %collective-permute-start.2 = (bf16[128,1152]{1,0:T(8,128)(2,1)}, bf16[128,1152]{1,0:T(8,128)(2,1)}, u32[]{:S(2)}, u32[]{:S(2)}) collective-permute-start(bf16[128,1152]{1,0:T(8,128)(2,1)} %copy-done.18), channel_id=1, source_target_pairs={{0,3},{1,0},{2,1},{3,2},{4,7},{5,4},{6,5},{7,6},{8,11},{9,8},{10,9... | collective-permute-start | bytes 884744 | tf_op jit(solution)/shard_map/ppermute | solution.py:45
  26.5 12.9 %collective-permute-start.1 = (bf16[128,1152]{1,0:T(8,128)(2,1)}, bf16[128,1152]{1,0:T(8,128)(2,1)}, u32[]{:S(2)}, u32[]{:S(2)}) collective-permute-start(bf16[128,1152]{1,0:T(8,128)(2,1)} %copy-done.18), channel_id=1, source_target_pairs={{0,2},{1,3},{2,0},{3,1},{4,6},{5,7},{6,4},{7,5},{8,10},{9,11},{10,... | collective-permute-start | bytes 884744 | tf_op jit(solution)/shard_map/ppermute | solution.py:45
  28.1 16.9 %collective-permute-start.6 = (bf16[128,1152]{1,0:T(8,128)(2,1)}, bf16[128,1152]{1,0:T(8,128)(2,1)}, u32[]{:S(2)}, u32[]{:S(2)}) collective-permute-start(bf16[128,1152]{1,0:T(8,128)(2,1)} %collective-permute-done.refs_4_), channel_id=1, source_target_pairs={{0,1},{1,2},{2,3},{3,0},{4,5},{5,6},{6,7},{7,4},{8,9},{9,10},{10,1... | collective-permute-start | bytes 884744 | tf_op jit(solution)/shard_map/ppermute | solution.py:45
  28.3 16.7 %collective-permute-start.5 = (bf16[128,1152]{1,0:T(8,128)(2,1)}, bf16[128,1152]{1,0:T(8,128)(2,1)}, u32[]{:S(2)}, u32[]{:S(2)}) collective-permute-start(bf16[128,1152]{1,0:T(8,128)(2,1)} %collective-permute-done.refs_4_), channel_id=1, source_target_pairs={{0,3},{1,0},{2,1},{3,2},{4,7},{5,4},{6,5},{7,6},{8,11},{9,8},{10,9... | collective-permute-start | bytes 884744 | tf_op jit(solution)/shard_map/ppermute | solution.py:45
  32.0 20.0 %collective-permute-start.4 = (bf16[128,1152]{1,0:T(8,128)(2,1)}, bf16[128,1152]{1,0:T(8,128)(2,1)}, u32[]{:S(2)}, u32[]{:S(2)}) collective-permute-start(bf16[128,1152]{1,0:T(8,128)(2,1)} %collective-permute-done.refs_4_), channel_id=1, source_target_pairs={{0,2},{1,3},{2,0},{3,1},{4,6},{5,7},{6,4},{7,5},{8,10},{9,11},{10,... | collective-permute-start | bytes 884744 | tf_op jit(solution)/shard_map/ppermute | solution.py:45
  52.9 6.4 %collective-permute-start.7 = (bf16[1024,1152]{1,0:T(8,128)(2,1)}, bf16[1024,1152]{1,0:T(8,128)(2,1)}, u32[]{:S(2)}, u32[]{:S(2)}) collective-permute-start(bf16[1024,1152]{1,0:T(8,128)(2,1)} %bitcast.refs_8_), channel_id=1, source_target_pairs={{0,8},{8,0},{1,9},{9,1},{2,10},{10,2},{3,11},{11,3},{4,12},{12,4},... | collective-permute-start | bytes 7077896 | tf_op jit(solution)/shard_map/ppermute | solution.py:53
  77.1 13.3 %collective-permute-start.11 = (bf16[1024,1152]{1,0:T(8,128)(2,1)}, bf16[1024,1152]{1,0:T(8,128)(2,1)S(1)}, u32[]{:S(2)}, u32[]{:S(2)}) collective-permute-start(bf16[1024,1152]{1,0:T(8,128)(2,1)} %get-tuple-element.48), channel_id=1, source_target_pairs={{0,8},{8,0},{1,9},{9,1},{2,10},{10,2},{3,11},{11,3},{4,12},{12,4},... | collective-permute-start | bytes 7077896 | tf_op jit(solution)/shard_map/ppermute | solution.py:53
  86.0 18.1 %collective-permute-start.8 = (bf16[256,1280]{1,0:T(8,128)(2,1)}, bf16[256,1280]{1,0:T(8,128)(2,1)}, u32[]{:S(2)}, u32[]{:S(2)}) collective-permute-start(bf16[256,1280]{1,0:T(8,128)(2,1)} %get-tuple-element.43), channel_id=1, source_target_pairs={{0,2},{1,3},{2,0},{3,1},{4,6},{5,7},{6,4},{7,5},{8,10},{9,11},{10,... | collective-permute-start | bytes 1966088 | tf_op jit(solution)/shard_map/ppermute | solution.py:49
  87.7 30.8 %collective-permute-start.9 = (bf16[256,1280]{1,0:T(8,128)(2,1)}, bf16[256,1280]{1,0:T(8,128)(2,1)}, u32[]{:S(2)}, u32[]{:S(2)}) collective-permute-start(bf16[256,1280]{1,0:T(8,128)(2,1)} %get-tuple-element.44), channel_id=1, source_target_pairs={{0,1},{1,2},{2,3},{3,0},{4,5},{5,6},{6,7},{7,4},{8,9},{9,10},{10,1... | collective-permute-start | bytes 1966088 | tf_op jit(solution)/shard_map/ppermute | solution.py:49
  88.2 30.3 %collective-permute-start.10 = (bf16[256,1280]{1,0:T(8,128)(2,1)}, bf16[256,1280]{1,0:T(8,128)(2,1)}, u32[]{:S(2)}, u32[]{:S(2)}) collective-permute-start(bf16[256,1280]{1,0:T(8,128)(2,1)} %get-tuple-element.45), channel_id=1, source_target_pairs={{0,3},{1,0},{2,1},{3,2},{4,7},{5,4},{6,5},{7,6},{8,11},{9,8},{10,9... | collective-permute-start | bytes 1966088 | tf_op jit(solution)/shard_map/ppermute | solution.py:49
  90.4 1.4 copy-start.17
  98.9 43.3 %all-to-all-start.1 = ((bf16[8,128,1152]{2,1,0:T(8,128)(2,1)}), bf16[8,128,1152]{2,1,0:T(8,128)(2,1)}, u32[]{:S(2)}, u32[]{:S(2)}) async-start(bf16[8,128,1152]{2,1,0:T(8,128)(2,1)} %bitcast.23), calls=%async_computation.1 | async-start | bytes 4718592 | tf_op jit(solution)/shard_map/all_to_all | solution.py:297
  120.7 1.1 copy-start.8
  121.7 19.0 %copy-start.22 = (f32[128]{0:T(128)S(1)}, f32[128]{0:T(128)}, u32[]{:S(2)}) copy-start(f32[128]{0:T(128)} %copy-done.21) | copy-start | bytes 1540
  122.5 16.1 %collective-permute-start.12 = (bf16[128,1280]{1,0:T(8,128)(2,1)}, bf16[128,1280]{1,0:T(8,128)(2,1)}, u32[]{:S(2)}, u32[]{:S(2)}) collective-permute-start(bf16[128,1280]{1,0:T(8,128)(2,1)} %slice.46), channel_id=1, source_target_pairs={{0,4},{4,0},{1,5},{5,1},{2,6},{6,2},{3,7},{7,3},{8,12},{12,8},{9,1... | collective-permute-start | bytes 983048 | tf_op jit(solution)/shard_map/ppermute | solution.py:53
  139.9 0.8 copy-start.7
  142.2 3.4 %copy-start.4 = (f32[128,1152]{1,0:T(8,128)S(1)}, f32[128,1152]{1,0:T(8,128)}, u32[]{:S(2)}) copy-start(f32[128,1152]{1,0:T(8,128)} %copy-done.3) | copy-start | bytes 1769476
  142.2 3.4 %copy-start.24 = (f32[128]{0:T(128)S(1)}, f32[128]{0:T(128)}, u32[]{:S(2)}) copy-start(f32[128]{0:T(128)} %copy-done.23) | copy-start | bytes 1540
  142.2 5.0 %copy-start.11 = (bf16[128,1152]{1,0:T(8,128)(2,1)S(1)}, bf16[128,1152]{1,0:T(8,128)(2,1)}, u32[]{:S(2)}) copy-start(bf16[128,1152]{1,0:T(8,128)(2,1)} %subtract_convert_fusion.1) | copy-start | bytes 884740
  142.3 5.0 %copy-start.14 = (bf16[128,1152]{1,0:T(8,128)(2,1)S(1)}, bf16[128,1152]{1,0:T(8,128)(2,1)}, u32[]{:S(2)}) copy-start(bf16[128,1152]{1,0:T(8,128)(2,1)} %copy-done.13) | copy-start | bytes 884740
  142.3 5.0 %copy-start.16 = (bf16[128,1152]{1,0:T(8,128)(2,1)S(1)}, bf16[128,1152]{1,0:T(8,128)(2,1)}, u32[]{:S(2)}) copy-start(bf16[128,1152]{1,0:T(8,128)(2,1)} %copy-done.15) | copy-start | bytes 884740
  146.5 0.7 copy-start.9
  147.4 3.3 %collective-permute-start.13 = (bf16[256,1152]{1,0:T(8,128)(2,1)S(1)}, bf16[256,1152]{1,0:T(8,128)(2,1)S(1)}, u32[]{:S(2)}, u32[]{:S(2)}) collective-permute-start(bf16[256,1152]{1,0:T(8,128)(2,1)S(1)} %get-tuple-element.60), channel_id=1, source_target_pairs={{0,8},{8,0},{1,9},{9,1},{2,10},{10,2},{3,11},{11,3},{4,12},{12,4},... | collective-permute-start | bytes 1769480 | tf_op jit(solution)/shard_map/ppermute | solution.py:53
  192.7 4.3 %collective-permute-start.16 = (bf16[72,1152]{1,0:T(8,128)(2,1)S(1)}, bf16[72,1152]{1,0:T(8,128)(2,1)S(1)}, u32[]{:S(2)}, u32[]{:S(2)}) collective-permute-start(bf16[72,1152]{1,0:T(8,128)(2,1)S(1)} %reduce_sum.152), channel_id=1, source_target_pairs={{0,68},{64,0},{4,64},{68,4},{1,69},{65,1},{5,65},{69,5},{2,70},{66... | collective-permute-start | bytes 497672 | tf_op jit(solution)/shard_map/ppermute | solution.py:269
  193.7 7.2 %collective-permute-start.15 = (bf16[72,1152]{1,0:T(8,128)(2,1)S(1)}, bf16[72,1152]{1,0:T(8,128)(2,1)S(1)}, u32[]{:S(2)}, u32[]{:S(2)}) collective-permute-start(bf16[72,1152]{1,0:T(8,128)(2,1)S(1)} %reduce_sum.152), channel_id=1, source_target_pairs={{0,64},{64,4},{4,68},{68,0},{1,65},{65,5},{5,69},{69,1},{2,66},{66... | collective-permute-start | bytes 497672 | tf_op jit(solution)/shard_map/ppermute | solution.py:269
  194.2 7.2 %collective-permute-start.14 = (bf16[72,1152]{1,0:T(8,128)(2,1)S(1)}, bf16[72,1152]{1,0:T(8,128)(2,1)S(1)}, u32[]{:S(2)}, u32[]{:S(2)}) collective-permute-start(bf16[72,1152]{1,0:T(8,128)(2,1)S(1)} %reduce_sum.152), channel_id=1, source_target_pairs={{0,4},{64,68},{4,0},{68,64},{1,5},{65,69},{5,1},{69,65},{2,6},{66,... | collective-permute-start | bytes 497672 | tf_op jit(solution)/shard_map/ppermute | solution.py:269
  201.8 40.9 %copy-start.5 = (bf16[128,1152]{1,0:T(8,128)(2,1)S(1)}, bf16[128,1152]{1,0:T(8,128)(2,1)}, u32[]{:S(2)}) copy-start(bf16[128,1152]{1,0:T(8,128)(2,1)} %param.6) | copy-start | bytes 884740
  201.8 40.8 %copy-start.12 = (bf16[128,1152]{1,0:T(8,128)(2,1)S(1)}, bf16[128,1152]{1,0:T(8,128)(2,1)}, u32[]{:S(2)}) copy-start(bf16[128,1152]{1,0:T(8,128)(2,1)} %subtract_convert_fusion.1) | copy-start | bytes 884740
  236.4 10.5 %collective-permute-start.17 = (bf16[1152,1152]{1,0:T(8,128)(2,1)S(1)}, bf16[1152,1152]{1,0:T(8,128)(2,1)S(1)}, u32[]{:S(2)}, u32[]{:S(2)}) collective-permute-start(bf16[1152,1152]{1,0:T(8,128)(2,1)S(1)} %bitcast.22), channel_id=1, source_target_pairs={{0,8},{8,0},{1,9},{9,1},{2,10},{10,2},{3,11},{11,3},{4,12},{12,4},... | collective-permute-start | bytes 7962632 | tf_op jit(solution)/shard_map/ppermute | solution.py:53
  242.6 2.1 copy-start.2
  242.6 2.1 copy-start.10
  242.6 2.1 copy-start.20

commit v3 on v2

--- a/solution.py
+++ b/solution.py
@@ -104,8 +104,8 @@
 def pair_kernel(n_img, rows, *refs):
     img_refs = refs[:n_img]
     txt_refs = refs[n_img : n_img + 2]
-    place_ref, temper_ref, offset_ref = refs[n_img + 2 : n_img + 5]
-    q_ref, loss_ref, images, texts, out_ref, even, odd, sems = refs[n_img + 5 :]
+    place_ref, img_place_ref, temper_ref, offset_ref = refs[n_img + 2 : n_img + 6]
+    out_ref, half_ref, grad_ref, q_ref, loss_ref, images, texts, total, even, odd, sems = refs[n_img + 6 :]
     n_txt = texts.shape[0] // rows
     moves = [(ref, images.at[pl.ds(at * rows, rows)]) for at, ref in enumerate(img_refs)]
     for at in range(n_txt):
@@ -149,31 +149,51 @@
     q_ref[:rows, :rows] = own_q
     loss_ref[:rows, :] += own_loss
     half = texts.shape[0] // 2
+    keep = pltpu.make_async_copy(q_ref.at[:, pl.ds(0, half)], half_ref, sems.at[0])
+    keep.start()
     for at in range(0, images.shape[1], WIDE):
         out_ref[:, at : at + WIDE] = lax.dot_general(
             q_ref[:, half:], images[:, at : at + WIDE], (((0,), (0,)), ((), ())), preferred_element_type=F32
         ).astype(BF)
-
-
-def pair_call(images, texts, place, temper, offset):
+    width = texts.shape[1]
+    for at in range(0, width, WIDE):
+        product = jnp.dot(q_ref[...], texts[:, at : at + WIDE], preferred_element_type=F32)
+        total[:, at : at + WIDE] = product.astype(BF)
+    total[:, width:] = loss_ref[...].astype(BF)
+    keep.wait()
+    moves = []
+    for at in range(n_img):
+        start = pl.multiple_of(img_place_ref[at] * rows, rows)
+        moves.append((total.at[pl.ds(at * rows, rows)], grad_ref.at[pl.ds(start, rows)]))
+    load_all(moves, sems)
+
+
+def pair_call(images, texts, place, img_place, temper, offset):
     rows, width = images[0].shape
     m, n = len(images) * rows, 2 * texts[0].shape[0]
     return pl.pallas_call(
         functools.partial(pair_kernel, len(images), rows),
-        in_specs=[HBM] * (len(images) + 2) + [SMEM] * 3,
-        out_specs=[VMEM] * 5,
+        in_specs=[HBM] * (len(images) + 2) + [SMEM] * 4,
+        out_specs=[VMEM] + [HBM] * 2,
         out_shape=[
+            pltpu.HBM((n // 2, width), BF),
+            pltpu.HBM((m, n // 2), BF),
+            pltpu.HBM((m, width + LANES), BF),
+        ],
+        scratch_shapes=[
             pltpu.VMEM((m, n), BF),
             pltpu.VMEM((m, LANES), F32),
             pltpu.VMEM((m, width), BF),
             pltpu.VMEM((n, width), BF),
-            pltpu.HBM((n // 2, width), BF),
+            pltpu.VMEM((m, width + LANES), BF),
+            pltpu.VMEM((m, TILE), F32),
+            pltpu.VMEM((m, TILE), F32),
+            pltpu.SemaphoreType.DMA((len(images) + n // rows,)),
         ],
-        scratch_shapes=[pltpu.VMEM((m, TILE), F32)] * 2 + [pltpu.SemaphoreType.DMA((len(images) + n // rows,))],
-        compiler_params=params(32),
-        cost_estimate=cost(4 * m * n * width, 10),
+        compiler_params=params(44),
+        cost_estimate=cost(6 * m * n * width, 16),
         name="pair",
-    )(*[in_hbm(block) for block in (*images, *texts)], place, temper, offset)
+    )(*[in_hbm(block) for block in (*images, *texts)], place, img_place, temper, offset)
 
 
 def cut_blocks(product, at, rows, out_refs, own_ref):
@@ -184,59 +204,46 @@
             ref[side * rows : (side + 1) * rows, columns] = block.astype(ref.dtype)
 
 
-def grad_img_kernel(rows, q_ref, texts, loss_ref, *refs):
-    width = texts.shape[1]
-    for at in range(0, width, WIDE):
-        product = jnp.dot(q_ref[...], texts[:, at : at + WIDE], preferred_element_type=F32)
-        cut_blocks(product, at, rows, refs[:3], refs[3])
-    cut_blocks(loss_ref[...], width, rows, refs[:3], refs[3])
-
-
-def grad_txt_kernel(rows, q_ref, images, got_ref, place_ref, out_ref, got, total, sems):
-    load_all([(got_ref, got)], sems)
+def grad_txt_kernel(n_img, rows, q_ref, *refs):
+    img_refs, got_ref, out_refs = refs[:n_img], refs[n_img], refs[n_img + 1 : n_img + 5]
+    q, images, got, sems = refs[n_img + 5 :]
+    moves = [(q_ref, q)] + [(ref, images.at[pl.ds(at * rows, rows)]) for at, ref in enumerate(img_refs)]
+    copies = [pltpu.make_async_copy(ref, into, sems.at[at]) for at, (ref, into) in enumerate(moves + [(got_ref, got)])]
+    for copy in copies:
+        copy.start()
+    for copy in copies[:-1]:
+        copy.wait()
     width = images.shape[1]
     for at in range(0, width, WIDE):
         product = lax.dot_general(
-            q_ref[:, : got.shape[0]], images[:, at : at + WIDE], (((0,), (0,)), ((), ())), preferred_element_type=F32
+            q[...], images[:, at : at + WIDE], (((0,), (0,)), ((), ())), preferred_element_type=F32
         )
-        total[:, at : at + WIDE] = (product + got[:, at : at + WIDE].astype(F32)).astype(BF)
-    blocks = got.shape[0] // rows
-    moves = []
-    for at in range(blocks):
-        start = pl.multiple_of(place_ref[at] * rows, rows)
-        moves.append((total.at[pl.ds(at * rows, rows)], out_ref.at[pl.ds(start, rows)]))
-    load_all(moves, sems)
+        if at == 0:
+            copies[-1].wait()
+        cut_blocks(product + got[:, at : at + WIDE].astype(F32), at, rows, out_refs[:3], out_refs[3])
 
 
 def cut_shapes(rows, width):
     return [pltpu.HBM((2 * rows, width), BF)] * 3 + [pltpu.HBM((2 * rows, width), F32)]
 
 
-def grad_img_call(q, texts, loss, rows):
-    width = texts.shape[1] + LANES
+def grad_txt_call(q, images, got, rows):
+    width = images[0].shape[1]
     return pl.pallas_call(
-        functools.partial(grad_img_kernel, rows),
-        in_specs=[VMEM] * 3,
+        functools.partial(grad_txt_kernel, len(images), rows),
+        in_specs=[HBM] * (2 + len(images)),
         out_specs=[VMEM] * 4,
         out_shape=cut_shapes(rows, width),
-        compiler_params=params(24),
-        cost_estimate=cost(2 * q.shape[0] * q.shape[1] * width, 4),
-        name="grad_img",
-    )(q, texts, loss)
-
-
-def grad_txt_call(q, images, got, place, rows):
-    width = images.shape[1]
-    return pl.pallas_call(
-        functools.partial(grad_txt_kernel, rows),
-        in_specs=[VMEM, VMEM, HBM, SMEM],
-        out_specs=HBM,
-        out_shape=pltpu.HBM(got.shape, BF),
-        scratch_shapes=[pltpu.VMEM(got.shape, BF)] * 2 + [pltpu.SemaphoreType.DMA((got.shape[0] // rows,))],
-        compiler_params=params(24),
+        scratch_shapes=[
+            pltpu.VMEM(q.shape, BF),
+            pltpu.VMEM((len(images) * rows, width), BF),
+            pltpu.VMEM(got.shape, BF),
+            pltpu.SemaphoreType.DMA((2 + len(images),)),
+        ],
+        compiler_params=params(32),
         cost_estimate=cost(2 * got.shape[0] * q.shape[0] * width, 6),
         name="grad_txt",
-    )(q, images, in_hbm(got), place)
+    )(*[in_hbm(value) for value in (q, *images, got)])
 
 
 def ring_give(parts, ring):
@@ -252,6 +259,12 @@
 def text_places():
     yl, z = lax.axis_index("yl"), lax.axis_index("z")
     places = [(yl ^ other) * 4 + (z + s) % 4 for other in (0, 1) for s in (0,) + STEPS]
+    return jnp.stack(places).astype(jnp.int32)
+
+
+def image_places():
+    yh, x = lax.axis_index("yh"), lax.axis_index("x")
+    places = [(yh ^ other) * 4 + (x + s) % 4 for other in (0, 1) for s in (0,) + STEPS]
     return jnp.stack(places).astype(jnp.int32)
 
 
@@ -289,15 +302,14 @@
     texts, images = lax.optimization_barrier((texts, images))
     texts = [texts, swap(texts, "c")]
     place = text_places()
-    q, loss, images, texts, sent = pair_call(images, texts, place, temper, offset)
+    sent, q_half, img_parts = pair_call(images, texts, place, image_places(), temper, offset)
     got = swap(sent, "c")
-    img_parts = ring_give(grad_img_call(q, texts, loss, rows), "x")
-    txt_parts = grad_txt_call(q, images, got, place, rows).reshape(8, rows, -1)
-    img_parts, _ = lax.optimization_barrier((img_parts, txt_parts))
-    txt_parts = lax.all_to_all(txt_parts, ("yl", "z"), 0, 0, tiled=True)
-    img_near, img_far = pair_sum(img_parts, "yh")
-    grad_img = img_near + img_far.astype(F32)
-    grad_txt = jnp.sum(txt_parts.astype(F32), 0)
+    img_parts = lax.all_to_all(img_parts.reshape(8, rows, -1), ("yh", "x"), 0, 0, tiled=True)
+    txt_parts = ring_give(grad_txt_call(q_half, images, got, rows), "z")
+    img_parts, txt_parts = lax.optimization_barrier((img_parts, txt_parts))
+    grad_img = jnp.sum(img_parts.astype(F32), 0)
+    txt_near, txt_far = pair_sum(txt_parts, "yl")
+    grad_txt = txt_near + txt_far.astype(F32)
     image_loss = jnp.sum(grad_img[:, img.shape[1] :], 1) * (1.0 / LOG2E)
     grad_img = grad_img[:, : img.shape[1]]
     image_gp = back_proj(image_state, grad_img).astype(BF)

time: 253 us -> 251 us (level)
  local copies, waits for them, and re-layouts: 7.79 us -> 3.79 us
  other arithmetic: 25.8 us -> 22.1 us
    all_to_all x1, waiting for transfers between devices: 0.01 us -> 20.5 us  [per_device(): lax.all_to_all(img_parts.reshape(8, rows, -1), ('yh', 'x'), 0, 0, tiled=T...]
    ppermute x3, waiting for transfers between devices: 15.2 us -> 3.59 us  [give(): return lax.ppermute(block, axis, [(i, (i + step) % 4) for i in range(4)])]
    pallas_call x1, Pallas kernels: 17.8 us -> 25.7 us  [pair_call(): pl.pallas_call(functools.partial(pair_kernel, len(images), rows), in_spec...]
    pallas_call x2 -> x1, Pallas kernels: 15.4 us -> 8.14 us  [grad_txt_call(): pl.pallas_call(functools.partial(grad_txt_kernel, len(images), rows), in_...]
    ppermute x6, waiting for transfers between devices: 21.7 us -> 14.9 us  [swap(): return lax.ppermute(block, axis, [(0, 1), (1, 0)])]
    unnamed x50 -> x54, local copies, waits for them, and re-layouts: 4.96 us -> 1.61 us
  transfers between devices with their start and end apart: 20 -> 20, of which waited for: 14 -> 13; matrix products, arithmetic and copies ran while one was open for 5% -> 3% of each run, Pallas kernels for 6% -> 3%
where the time goes in v3:
time: 251 us
  blocking collectives  74.6 us (30%)
  waiting for transfers between devices  66.3 us (26%)
  starting transfers between devices  43.2 us (17%)
  Pallas kernels  33.9 us (14%)
  other arithmetic  22.1 us (9%)
  matrix products  4.44 us (2%)
  local copies, waits for them, and re-layouts  3.79 us (2%)
    all_to_all x1, blocking collectives, reduce_weights(): lax.all_to_all(part.astype(BF).reshape(16, rows // 16, cols), ('z', 'x'),...  40.5 us
    all_to_all x1, blocking collectives, reduce_weights(): lax.all_to_all(jnp.broadcast_to(total[None], (16,) + total.shape), ('z',...  34.1 us
    pallas_call x1, Pallas kernels, pair_call(): pl.pallas_call(functools.partial(pair_kernel, len(images), rows), in_spec...  25.7 us
    all_to_all x1, waiting for transfers between devices, per_device(): lax.all_to_all(img_parts.reshape(8, rows, -1), ('yh', 'x'), 0, 0, tiled=T...  20.5 us
    ppermute x6, waiting for transfers between devices, fetch(): return lax.ppermute(block, axis, [(i, (i - step) % 4) for i in range(4)])  19.8 us
    ppermute x6, waiting for transfers between devices, swap(): return lax.ppermute(block, axis, [(0, 1), (1, 0)])  14.9 us
    ppermute x6, starting transfers between devices, swap(): return lax.ppermute(block, axis, [(0, 1), (1, 0)])  13.6 us
    ppermute x6, starting transfers between devices, fetch(): return lax.ppermute(block, axis, [(i, (i - step) % 4) for i in range(4)])  8.42 us
  transfers between devices with their start and end apart: 20, of which 13 were waited for; matrix products, arithmetic and copies ran while one was open for 3% of the time, Pallas kernels for 3%

profile of v3, /device:TPU:1, one launch (start us, length us, event | category | flops | bytes accessed | tf_op | source)
XLA Modules:
  0.0 250.8 jit_solution(15093759372868037829)
XLA Ops:
  0.6 1.2 convert_reduce_fusion.2
  1.9 1.2 fusion.17
  3.6 1.2 fusion.4
  6.2 3.8 %collective-permute-start = (bf16[128,1152]{1,0:T(8,128)(2,1)S(1)}, bf16[128,1152]{1,0:T(8,128)(2,1)}, u32[]{:S(2)}, u32[]{:S(2)}) collective-permute-start(bf16[128,1152]{1,0:T(8,128)(2,1)S(1)} %multiply_convert_fusion.1.refs_0_), channel_id=1, source_target_pairs={{0,4},{4,0},{1,5},{5,1},{2,6},{6,2},{3,7},{7,3},{8,12},{12,8},{9,1... | collective-permute-start | bytes 884744 | tf_op jit(solution)/shard_map/ppermute | solution.py:53
  13.0 3.5 %collective-permute-done.refs_4_ = bf16[128,1152]{1,0:T(8,128)(2,1)} collective-permute-done((bf16[128,1152]{1,0:T(8,128)(2,1)S(1)}, bf16[128,1152]{1,0:T(8,128)(2,1)}, u32[]{:S(2)}, u32[]{:S(2)}) %collective-permute-start) | collective-permute-done | bytes 294944 | tf_op jit(solution)/shard_map/ppermute | solution.py:53
  16.6 1.7 broadcast_in_dim.4
  18.3 6.0 %all-to-all-start = ((bf16[8,128,1152]{2,1,0:T(8,128)(2,1)}), bf16[8,128,1152]{2,1,0:T(8,128)(2,1)}, u32[]{:S(2)}, u32[]{:S(2)}) async-start(bf16[8,128,1152]{2,1,0:T(8,128)(2,1)} %broadcast_in_dim.4), calls=%async_computation | async-start | bytes 4718592 | tf_op jit(solution)/shard_map/all_to_all | solution.py:273
  24.3 1.2 collective-permute-start.3
  25.6 1.4 collective-permute-start.2
  27.0 1.5 collective-permute-start.1
  28.9 2.4 collective-permute-start.5
  31.2 1.3 collective-permute-done.3.refs_3_
  32.5 1.5 collective-permute-start.4
  34.1 5.8 %collective-permute-done.1.refs_1_ = bf16[128,1152]{1,0:T(8,128)(2,1)} collective-permute-done((bf16[128,1152]{1,0:T(8,128)(2,1)}, bf16[128,1152]{1,0:T(8,128)(2,1)}, u32[]{:S(2)}, u32[]{:S(2)}) %collective-permute-start.1) | collective-permute-done | bytes 294944 | tf_op jit(solution)/shard_map/ppermute | solution.py:45
  39.9 5.6 %collective-permute-done.6.refs_7_ = bf16[128,1152]{1,0:T(8,128)(2,1)} collective-permute-done((bf16[128,1152]{1,0:T(8,128)(2,1)}, bf16[128,1152]{1,0:T(8,128)(2,1)}, u32[]{:S(2)}, u32[]{:S(2)}) %collective-permute-start.6) | collective-permute-done | bytes 294944 | tf_op jit(solution)/shard_map/ppermute | solution.py:45
  45.5 7.0 %collective-permute-done.4.refs_5_ = bf16[128,1152]{1,0:T(8,128)(2,1)} collective-permute-done((bf16[128,1152]{1,0:T(8,128)(2,1)}, bf16[128,1152]{1,0:T(8,128)(2,1)}, u32[]{:S(2)}, u32[]{:S(2)}) %collective-permute-start.4) | collective-permute-done | bytes 294944 | tf_op jit(solution)/shard_map/ppermute | solution.py:45
  52.5 0.9 all-to-all-done
  53.4 1.9 collective-permute-start.7
  56.7 3.0 %collective-permute-done.7.refs_9_ = bf16[1024,1152]{1,0:T(8,128)(2,1)} collective-permute-done((bf16[1024,1152]{1,0:T(8,128)(2,1)}, bf16[1024,1152]{1,0:T(8,128)(2,1)}, u32[]{:S(2)}, u32[]{:S(2)}) %collective-permute-start.7) | collective-permute-done | bytes 2359328 | tf_op jit(solution)/shard_map/ppermute | solution.py:53
  59.8 25.7 %pair.1 = (bf16[1024,1152]{1,0:T(8,128)(2,1)}, bf16[1024,1024]{1,0:T(8,128)(2,1)}, bf16[1024,1280]{1,0:T(8,128)(2,1)}) custom-call(bf16[128,1152]{1,0:T(8,128)(2,1)} %copy-done.16, bf16[128,1152]{1,0:T(8,128)(2,1)} %collective-permute-done.1.refs_1_, bf16[128,1152]{1,0:T(8,128)(2,1)} %collective-permute-done.2.refs_2_, ...), custom_call_target="tpu_custom_call" | custom-call | flops 14495514624 | bytes 16777216 | tf_op jit(solution)/shard_map/pair/pallas_call | solution.py:174
  86.0 5.3 %all-to-all-start.1 = ((bf16[8,128,1280]{2,1,0:T(8,128)(2,1)}), bf16[8,128,1280]{2,1,0:T(8,128)(2,1)}, u32[]{:S(2)}, u32[]{:S(2)}) async-start(bf16[8,128,1280]{2,1,0:T(8,128)(2,1)} %bitcast.32), calls=%async_computation.1 | async-start | bytes 5242880 | tf_op jit(solution)/shard_map/all_to_all | solution.py:307
  91.3 8.1 %grad_txt.1 = (bf16[256,1152]{1,0:T(8,128)(2,1)}, bf16[256,1152]{1,0:T(8,128)(2,1)}, bf16[256,1152]{1,0:T(8,128)(2,1)}, f32[256,1152]{1,0:T(8,128)}) custom-call(bf16[1024,1024]{1,0:T(8,128)(2,1)} %get-tuple-element.40.q_ref, bf16[128,1152]{1,0:T(8,128)(2,1)} %copy-done.16, bf16[128,1152]{1,0:T(8,128)(2,1)} %collective-permute-done.1.refs_1_, ...), custom_call_target="tpu_custom_call" | custom-call | flops 2415919104 | bytes 6291456 | tf_op jit(solution)/shard_map/grad_txt/pallas_call | solution.py:232
  99.4 3.0 %collective-permute-start.9 = (bf16[256,1152]{1,0:T(8,128)(2,1)}, bf16[256,1152]{1,0:T(8,128)(2,1)}, u32[]{:S(2)}, u32[]{:S(2)}) collective-permute-start(bf16[256,1152]{1,0:T(8,128)(2,1)} %get-tuple-element.42), channel_id=1, source_target_pairs={{0,32},{16,48},{32,0},{48,16},{1,33},{17,49},{33,1},{49,17},{2,34}... | collective-permute-start | bytes 1769480 | tf_op jit(solution)/shard_map/ppermute | solution.py:49
  102.7 2.4 collective-permute-start.11
  105.1 20.5 %all-to-all-done.1 = bf16[8,128,1280]{2,1,0:T(8,128)(2,1)} async-done(((bf16[8,128,1280]{2,1,0:T(8,128)(2,1)}), bf16[8,128,1280]{2,1,0:T(8,128)(2,1)}, u32[]{:S(2)}, u32[]{:S(2)}) %all-to-all-start.1) | async-done | bytes 2621472 | tf_op jit(solution)/shard_map/all_to_all | solution.py:307
  125.6 3.6 %collective-permute-done.10 = bf16[256,1152]{1,0:T(8,128)(2,1)} collective-permute-done((bf16[256,1152]{1,0:T(8,128)(2,1)}, bf16[256,1152]{1,0:T(8,128)(2,1)}, u32[]{:S(2)}, u32[]{:S(2)}) %collective-permute-start.10) | collective-permute-done | bytes 589856 | tf_op jit(solution)/shard_map/ppermute | solution.py:49
  129.2 2.2 convert_reduce_fusion
  131.6 1.8 add_add_fusion
  133.5 0.9 collective-permute-start.12
  134.6 6.8 %collective-permute-done.12 = bf16[128,1152]{1,0:T(8,128)(2,1)S(1)} collective-permute-done((bf16[128,1152]{1,0:T(8,128)(2,1)S(1)}, bf16[128,1152]{1,0:T(8,128)(2,1)S(1)}, u32[]{:S(2)}, u32[]{:S(2)}) %collective-permute-start.12) | collective-permute-done | bytes 294944 | tf_op jit(solution)/shard_map/ppermute | solution.py:53
  141.9 1.7 collective-permute-start.13
  143.7 1.6 collective-permute-done.13
  145.4 1.0 convolution_convert_fusion
  146.4 40.5 %all_to_all.20 = bf16[16,72,1152]{2,1,0:T(8,128)(2,1)} all-to-all(bf16[16,72,1152]{2,1,0:T(8,128)(2,1)S(1)} %bitcast.31), channel_id=1, replica_groups=mesh['yl'=2,'z'=4,'c'=2,'yh'=2,'x'=4] {'z','x'}, dimensions={0} | all-to-all | bytes 5308416 | tf_op jit(solution)/shard_map/all_to_all | solution.py:278
  186.9 2.2 reduce_sum.152
  189.1 2.8 %collective-permute-start.16 = (bf16[72,1152]{1,0:T(8,128)(2,1)S(1)}, bf16[72,1152]{1,0:T(8,128)(2,1)S(1)}, u32[]{:S(2)}, u32[]{:S(2)}) collective-permute-start(bf16[72,1152]{1,0:T(8,128)(2,1)S(1)} %reduce_sum.152), channel_id=1, source_target_pairs={{0,68},{64,0},{4,64},{68,4},{1,69},{65,1},{5,65},{69,5},{2,70},{66... | collective-permute-start | bytes 497672 | tf_op jit(solution)/shard_map/ppermute | solution.py:282
  191.8 1.5 collective-permute-start.14
  193.3 0.8 collective-permute-done.16
  194.1 5.8 %collective-permute-done.15 = bf16[72,1152]{1,0:T(8,128)(2,1)S(1)} collective-permute-done((bf16[72,1152]{1,0:T(8,128)(2,1)S(1)}, bf16[72,1152]{1,0:T(8,128)(2,1)S(1)}, u32[]{:S(2)}, u32[]{:S(2)}) %collective-permute-start.15) | collective-permute-done | bytes 165920 | tf_op jit(solution)/shard_map/ppermute | solution.py:282
  199.9 1.0 add_convert_fusion
  201.2 34.1 %all_to_all.21 = bf16[16,72,1152]{2,1,0:T(8,128)(2,1)S(1)} all-to-all(bf16[16,72,1152]{2,1,0:T(8,128)(2,1)S(1)} %broadcast_in_dim.5), channel_id=1, replica_groups=mesh['yl'=2,'z'=4,'c'=2,'yh'=2,'x'=4] {'z','x'}, dimensions={0} | all-to-all | bytes 5308416 | tf_op jit(solution)/shard_map/all_to_all | solution.py:284
  235.2 4.8 %collective-permute-start.17 = (bf16[1152,1152]{1,0:T(8,128)(2,1)S(1)}, bf16[1152,1152]{1,0:T(8,128)(2,1)S(1)}, u32[]{:S(2)}, u32[]{:S(2)}) collective-permute-start(bf16[1152,1152]{1,0:T(8,128)(2,1)S(1)} %bitcast.30), channel_id=1, source_target_pairs={{0,8},{8,0},{1,9},{9,1},{2,10},{10,2},{3,11},{11,3},{4,12},{12,4},... | collective-permute-start | bytes 7962632 | tf_op jit(solution)/shard_map/ppermute | solution.py:53
  240.0 0.9 slice_reduce_fusion
  241.5 1.0 fusion.26
  242.6 1.1 fusion.16
  243.6 1.0 fusion.25
  244.7 1.1 fusion.12
  245.8 5.0 %select_convert_fusion = (f32[1152,1152]{1,0:T(8,128)}, f32[1152,1152]{1,0:T(8,128)}) fusion(bf16[1152,1152]{1,0:T(8,128)(2,1)S(1)} %collective-permute-done.17, pred[]{:T(512)S(6)} %eq.23, bf16[16,72,1152]{2,1,0:T(8,128)(2,1)S(1)} %all_to_all.21), kind=kLoop, calls=%fused_computation.2 | loop fusion | flops 5308416 | bytes 15925249 | tf_op jit(solution)/shard_map/convert_element_type | solution.py:327
  (92 shorter events, 7.8 us)
Async XLA Ops:
  0.6 4.2 %copy-start = (bf16[1152,1152]{1,0:T(8,128)(2,1)S(1)}, bf16[1152,1152]{1,0:T(8,128)(2,1)}, u32[]{:S(2)}) copy-start(bf16[1152,1152]{1,0:T(8,128)(2,1)} %param.8) | copy-start | bytes 7962628
  1.9 8.1 %copy-start.6 = (bf16[128,1152]{1,0:T(8,128)(2,1)S(1)}, bf16[128,1152]{1,0:T(8,128)(2,1)}, u32[]{:S(2)}) copy-start(bf16[128,1152]{1,0:T(8,128)(2,1)} %param.7) | copy-start | bytes 884740
  3.1 0.5 copy-start.17
  4.8 5.6 %copy-start.10 = (bf16[128,1152]{1,0:T(8,128)(2,1)}, bf16[128,1152]{1,0:T(8,128)(2,1)S(1)}, u32[]{:S(2)}) copy-start(bf16[128,1152]{1,0:T(8,128)(2,1)S(1)} %fusion.4) | copy-start | bytes 884740
  4.8 6.3 %copy-start.1 = (bf16[1152,1152]{1,0:T(8,128)(2,1)S(1)}, bf16[1152,1152]{1,0:T(8,128)(2,1)}, u32[]{:S(2)}) copy-start(bf16[1152,1152]{1,0:T(8,128)(2,1)} %param.9) | copy-start | bytes 7962628
  6.1 4.3 %copy-start.21 = (f32[128]{0:T(128)}, f32[128]{0:T(128)S(1)}, u32[]{:S(2)}) copy-start(f32[128]{0:T(128)S(1)} %get-tuple-element.66) | copy-start | bytes 1540
  6.2 6.6 %copy-start.16 = (bf16[128,1152]{1,0:T(8,128)(2,1)}, bf16[128,1152]{1,0:T(8,128)(2,1)S(1)}, u32[]{:S(2)}) copy-start(bf16[128,1152]{1,0:T(8,128)(2,1)S(1)} %multiply_convert_fusion.1.refs_0_) | copy-start | bytes 884740
  6.2 10.4 %collective-permute-start = (bf16[128,1152]{1,0:T(8,128)(2,1)S(1)}, bf16[128,1152]{1,0:T(8,128)(2,1)}, u32[]{:S(2)}, u32[]{:S(2)}) collective-permute-start(bf16[128,1152]{1,0:T(8,128)(2,1)S(1)} %multiply_convert_fusion.1.refs_0_), channel_id=1, source_target_pairs={{0,4},{4,0},{1,5},{5,1},{2,6},{6,2},{3,7},{7,3},{8,12},{12,8},{9,1... | collective-permute-start | bytes 884744 | tf_op jit(solution)/shard_map/ppermute | solution.py:53
  10.4 0.5 copy-start.19
  11.2 1.6 copy-start.12
  11.9 0.8 copy-start.3
  12.5 0.6 copy-start.23
  18.3 35.1 %all-to-all-start = ((bf16[8,128,1152]{2,1,0:T(8,128)(2,1)}), bf16[8,128,1152]{2,1,0:T(8,128)(2,1)}, u32[]{:S(2)}, u32[]{:S(2)}) async-start(bf16[8,128,1152]{2,1,0:T(8,128)(2,1)} %broadcast_in_dim.4), calls=%async_computation | async-start | bytes 4718592 | tf_op jit(solution)/shard_map/all_to_all | solution.py:273
  24.3 8.2 %collective-permute-start.3 = (bf16[128,1152]{1,0:T(8,128)(2,1)}, bf16[128,1152]{1,0:T(8,128)(2,1)}, u32[]{:S(2)}, u32[]{:S(2)}) collective-permute-start(bf16[128,1152]{1,0:T(8,128)(2,1)} %copy-done.16), channel_id=1, source_target_pairs={{0,1},{1,2},{2,3},{3,0},{4,5},{5,6},{6,7},{7,4},{8,9},{9,10},{10,1... | collective-permute-start | bytes 884744 | tf_op jit(solution)/shard_map/ppermute | solution.py:45
  25.6 8.5 %collective-permute-start.2 = (bf16[128,1152]{1,0:T(8,128)(2,1)}, bf16[128,1152]{1,0:T(8,128)(2,1)}, u32[]{:S(2)}, u32[]{:S(2)}) collective-permute-start(bf16[128,1152]{1,0:T(8,128)(2,1)} %copy-done.16), channel_id=1, source_target_pairs={{0,3},{1,0},{2,1},{3,2},{4,7},{5,4},{6,5},{7,6},{8,11},{9,8},{10,9... | collective-permute-start | bytes 884744 | tf_op jit(solution)/shard_map/ppermute | solution.py:45
  27.0 12.9 %collective-permute-start.1 = (bf16[128,1152]{1,0:T(8,128)(2,1)}, bf16[128,1152]{1,0:T(8,128)(2,1)}, u32[]{:S(2)}, u32[]{:S(2)}) collective-permute-start(bf16[128,1152]{1,0:T(8,128)(2,1)} %copy-done.16), channel_id=1, source_target_pairs={{0,2},{1,3},{2,0},{3,1},{4,6},{5,7},{6,4},{7,5},{8,10},{9,11},{10,... | collective-permute-start | bytes 884744 | tf_op jit(solution)/shard_map/ppermute | solution.py:45
  28.5 16.9 %collective-permute-start.6 = (bf16[128,1152]{1,0:T(8,128)(2,1)}, bf16[128,1152]{1,0:T(8,128)(2,1)}, u32[]{:S(2)}, u32[]{:S(2)}) collective-permute-start(bf16[128,1152]{1,0:T(8,128)(2,1)} %collective-permute-done.refs_4_), channel_id=1, source_target_pairs={{0,1},{1,2},{2,3},{3,0},{4,5},{5,6},{6,7},{7,4},{8,9},{9,10},{10,1... | collective-permute-start | bytes 884744 | tf_op jit(solution)/shard_map/ppermute | solution.py:45
  28.9 16.6 %collective-permute-start.5 = (bf16[128,1152]{1,0:T(8,128)(2,1)}, bf16[128,1152]{1,0:T(8,128)(2,1)}, u32[]{:S(2)}, u32[]{:S(2)}) collective-permute-start(bf16[128,1152]{1,0:T(8,128)(2,1)} %collective-permute-done.refs_4_), channel_id=1, source_target_pairs={{0,3},{1,0},{2,1},{3,2},{4,7},{5,4},{6,5},{7,6},{8,11},{9,8},{10,9... | collective-permute-start | bytes 884744 | tf_op jit(solution)/shard_map/ppermute | solution.py:45
  32.5 20.0 %collective-permute-start.4 = (bf16[128,1152]{1,0:T(8,128)(2,1)}, bf16[128,1152]{1,0:T(8,128)(2,1)}, u32[]{:S(2)}, u32[]{:S(2)}) collective-permute-start(bf16[128,1152]{1,0:T(8,128)(2,1)} %collective-permute-done.refs_4_), channel_id=1, source_target_pairs={{0,2},{1,3},{2,0},{3,1},{4,6},{5,7},{6,4},{7,5},{8,10},{9,11},{10,... | collective-permute-start | bytes 884744 | tf_op jit(solution)/shard_map/ppermute | solution.py:45
  53.4 6.4 %collective-permute-start.7 = (bf16[1024,1152]{1,0:T(8,128)(2,1)}, bf16[1024,1152]{1,0:T(8,128)(2,1)}, u32[]{:S(2)}, u32[]{:S(2)}) collective-permute-start(bf16[1024,1152]{1,0:T(8,128)(2,1)} %bitcast.refs_8_), channel_id=1, source_target_pairs={{0,8},{8,0},{1,9},{9,1},{2,10},{10,2},{3,11},{11,3},{4,12},{12,4},... | collective-permute-start | bytes 7077896 | tf_op jit(solution)/shard_map/ppermute | solution.py:53
  85.5 5.8 %collective-permute-start.8 = (bf16[1024,1152]{1,0:T(8,128)(2,1)}, bf16[1024,1152]{1,0:T(8,128)(2,1)}, u32[]{:S(2)}, u32[]{:S(2)}) collective-permute-start(bf16[1024,1152]{1,0:T(8,128)(2,1)} %get-tuple-element.41), channel_id=1, source_target_pairs={{0,8},{8,0},{1,9},{9,1},{2,10},{10,2},{3,11},{11,3},{4,12},{12,4},... | collective-permute-start | bytes 7077896 | tf_op jit(solution)/shard_map/ppermute | solution.py:53
  86.0 39.7 %all-to-all-start.1 = ((bf16[8,128,1280]{2,1,0:T(8,128)(2,1)}), bf16[8,128,1280]{2,1,0:T(8,128)(2,1)}, u32[]{:S(2)}, u32[]{:S(2)}) async-start(bf16[8,128,1280]{2,1,0:T(8,128)(2,1)} %bitcast.32), calls=%async_computation.1 | async-start | bytes 5242880 | tf_op jit(solution)/shard_map/all_to_all | solution.py:307
  99.4 26.2 %collective-permute-start.9 = (bf16[256,1152]{1,0:T(8,128)(2,1)}, bf16[256,1152]{1,0:T(8,128)(2,1)}, u32[]{:S(2)}, u32[]{:S(2)}) collective-permute-start(bf16[256,1152]{1,0:T(8,128)(2,1)} %get-tuple-element.42), channel_id=1, source_target_pairs={{0,32},{16,48},{32,0},{48,16},{1,33},{17,49},{33,1},{49,17},{2,34}... | collective-permute-start | bytes 1769480 | tf_op jit(solution)/shard_map/ppermute | solution.py:49
  102.4 26.8 %collective-permute-start.10 = (bf16[256,1152]{1,0:T(8,128)(2,1)}, bf16[256,1152]{1,0:T(8,128)(2,1)}, u32[]{:S(2)}, u32[]{:S(2)}) collective-permute-start(bf16[256,1152]{1,0:T(8,128)(2,1)} %get-tuple-element.43), channel_id=1, source_target_pairs={{0,16},{16,32},{32,48},{48,0},{1,17},{17,33},{33,49},{49,1},{2,18}... | collective-permute-start | bytes 1769480 | tf_op jit(solution)/shard_map/ppermute | solution.py:49
  102.7 26.5 %collective-permute-start.11 = (bf16[256,1152]{1,0:T(8,128)(2,1)}, bf16[256,1152]{1,0:T(8,128)(2,1)}, u32[]{:S(2)}, u32[]{:S(2)}) collective-permute-start(bf16[256,1152]{1,0:T(8,128)(2,1)} %get-tuple-element.44), channel_id=1, source_target_pairs={{0,48},{16,0},{32,16},{48,32},{1,49},{17,1},{33,17},{49,33},{2,50}... | collective-permute-start | bytes 1769480 | tf_op jit(solution)/shard_map/ppermute | solution.py:49
  125.6 6.0 %copy-start.14 = (f32[256,1152]{1,0:T(8,128)S(1)}, f32[256,1152]{1,0:T(8,128)}, u32[]{:S(2)}) copy-start(f32[256,1152]{1,0:T(8,128)} %get-tuple-element.50) | copy-start | bytes 3538948
  131.4 3.0 %copy-start.7 = (f32[128,1280]{1,0:T(8,128)}, f32[128,1280]{1,0:T(8,128)S(1)}, u32[]{:S(2)}) copy-start(f32[128,1280]{1,0:T(8,128)S(1)} %convert_reduce_fusion) | copy-start | bytes 1966084
  131.6 2.8 %copy-start.22 = (f32[128]{0:T(128)S(1)}, f32[128]{0:T(128)}, u32[]{:S(2)}) copy-start(f32[128]{0:T(128)} %copy-done.21) | copy-start | bytes 1540
  131.6 2.8 %copy-start.25 = (f32[128]{0:T(128)S(1)}, f32[128]{0:T(128)}, u32[]{:S(2)}) copy-start(f32[128]{0:T(128)} %get-tuple-element.65) | copy-start | bytes 1540
  131.6 9.7 %copy-start.4 = (f32[128,1152]{1,0:T(8,128)S(1)}, f32[128,1152]{1,0:T(8,128)}, u32[]{:S(2)}) copy-start(f32[128,1152]{1,0:T(8,128)} %copy-done.3) | copy-start | bytes 1769476
  133.4 8.1 %copy-start.24 = (f32[128]{0:T(128)S(1)}, f32[128]{0:T(128)}, u32[]{:S(2)}) copy-start(f32[128]{0:T(128)} %copy-done.23) | copy-start | bytes 1540
  133.4 8.1 %copy-start.26 = (f32[128]{0:T(128)S(1)}, f32[128]{0:T(128)}, u32[]{:S(2)}) copy-start(f32[128]{0:T(128)} %get-tuple-element.63) | copy-start | bytes 1540
  133.4 8.3 %copy-start.11 = (bf16[128,1152]{1,0:T(8,128)(2,1)S(1)}, bf16[128,1152]{1,0:T(8,128)(2,1)}, u32[]{:S(2)}) copy-start(bf16[128,1152]{1,0:T(8,128)(2,1)} %copy-done.10) | copy-start | bytes 884740
  133.4 8.3 %copy-start.13 = (bf16[128,1152]{1,0:T(8,128)(2,1)S(1)}, bf16[128,1152]{1,0:T(8,128)(2,1)}, u32[]{:S(2)}) copy-start(bf16[128,1152]{1,0:T(8,128)(2,1)} %copy-done.12) | copy-start | bytes 884740
  133.5 7.9 %collective-permute-start.12 = (bf16[128,1152]{1,0:T(8,128)(2,1)S(1)}, bf16[128,1152]{1,0:T(8,128)(2,1)S(1)}, u32[]{:S(2)}, u32[]{:S(2)}) collective-permute-start(bf16[128,1152]{1,0:T(8,128)(2,1)S(1)} %slice.50), channel_id=1, source_target_pairs={{0,64},{64,0},{1,65},{65,1},{2,66},{66,2},{3,67},{67,3},{4,68},{68... | collective-permute-start | bytes 884744 | tf_op jit(solution)/shard_map/ppermute | solution.py:53
  134.6 7.4 %copy-start.8 = (bf16[128,1152]{1,0:T(8,128)(2,1)}, bf16[128,1152]{1,0:T(8,128)(2,1)S(1)}, u32[]{:S(2)}) copy-start(bf16[128,1152]{1,0:T(8,128)(2,1)S(1)} %subtract_convert_fusion.1) | copy-start | bytes 884740
  141.9 3.4 %collective-permute-start.13 = (bf16[256,1152]{1,0:T(8,128)(2,1)S(1)}, bf16[256,1152]{1,0:T(8,128)(2,1)S(1)}, u32[]{:S(2)}, u32[]{:S(2)}) collective-permute-start(bf16[256,1152]{1,0:T(8,128)(2,1)S(1)} %get-tuple-element.58), channel_id=1, source_target_pairs={{0,8},{8,0},{1,9},{9,1},{2,10},{10,2},{3,11},{11,3},{4,12},{12,4},... | collective-permute-start | bytes 1769480 | tf_op jit(solution)/shard_map/ppermute | solution.py:53
  189.1 10.9 %copy-start.15 = (bf16[72,1152]{1,0:T(8,128)(2,1)}, bf16[72,1152]{1,0:T(8,128)(2,1)S(1)}, u32[]{:S(2)}) copy-start(bf16[72,1152]{1,0:T(8,128)(2,1)S(1)} %reduce_sum.152) | copy-start | bytes 497668
  189.1 5.0 %collective-permute-start.16 = (bf16[72,1152]{1,0:T(8,128)(2,1)S(1)}, bf16[72,1152]{1,0:T(8,128)(2,1)S(1)}, u32[]{:S(2)}, u32[]{:S(2)}) collective-permute-start(bf16[72,1152]{1,0:T(8,128)(2,1)S(1)} %reduce_sum.152), channel_id=1, source_target_pairs={{0,68},{64,0},{4,64},{68,4},{1,69},{65,1},{5,65},{69,5},{2,70},{66... | collective-permute-start | bytes 497672 | tf_op jit(solution)/shard_map/ppermute | solution.py:282
  191.8 8.1 %collective-permute-start.15 = (bf16[72,1152]{1,0:T(8,128)(2,1)S(1)}, bf16[72,1152]{1,0:T(8,128)(2,1)S(1)}, u32[]{:S(2)}, u32[]{:S(2)}) collective-permute-start(bf16[72,1152]{1,0:T(8,128)(2,1)S(1)} %reduce_sum.152), channel_id=1, source_target_pairs={{0,64},{64,4},{4,68},{68,0},{1,65},{65,5},{5,69},{69,1},{2,66},{66... | collective-permute-start | bytes 497672 | tf_op jit(solution)/shard_map/ppermute | solution.py:282
  191.8 8.1 %collective-permute-start.14 = (bf16[72,1152]{1,0:T(8,128)(2,1)S(1)}, bf16[72,1152]{1,0:T(8,128)(2,1)S(1)}, u32[]{:S(2)}, u32[]{:S(2)}) collective-permute-start(bf16[72,1152]{1,0:T(8,128)(2,1)S(1)} %reduce_sum.152), channel_id=1, source_target_pairs={{0,4},{64,68},{4,0},{68,64},{1,5},{65,69},{5,1},{69,65},{2,6},{66,... | collective-permute-start | bytes 497672 | tf_op jit(solution)/shard_map/ppermute | solution.py:282
  201.1 40.3 %copy-start.5 = (bf16[128,1152]{1,0:T(8,128)(2,1)S(1)}, bf16[128,1152]{1,0:T(8,128)(2,1)}, u32[]{:S(2)}) copy-start(bf16[128,1152]{1,0:T(8,128)(2,1)} %param.6) | copy-start | bytes 884740
  201.2 40.3 %copy-start.9 = (bf16[128,1152]{1,0:T(8,128)(2,1)S(1)}, bf16[128,1152]{1,0:T(8,128)(2,1)}, u32[]{:S(2)}) copy-start(bf16[128,1152]{1,0:T(8,128)(2,1)} %copy-done.8) | copy-start | bytes 884740
  201.2 40.3 %copy-start.18 = (f32[128]{0:T(128)S(1)}, f32[128]{0:T(128)}, u32[]{:S(2)}) copy-start(f32[128]{0:T(128)} %copy-done.17) | copy-start | bytes 1540
  235.2 10.5 %collective-permute-start.17 = (bf16[1152,1152]{1,0:T(8,128)(2,1)S(1)}, bf16[1152,1152]{1,0:T(8,128)(2,1)S(1)}, u32[]{:S(2)}, u32[]{:S(2)}) collective-permute-start(bf16[1152,1152]{1,0:T(8,128)(2,1)S(1)} %bitcast.30), channel_id=1, source_target_pairs={{0,8},{8,0},{1,9},{9,1},{2,10},{10,2},{3,11},{11,3},{4,12},{12,4},... | collective-permute-start | bytes 7962632 | tf_op jit(solution)/shard_map/ppermute | solution.py:53
  241.5 2.1 copy-start.2
  241.5 2.1 copy-start.20

commit v4 on v3

--- a/solution.py
+++ b/solution.py
@@ -118,7 +118,7 @@
     loss_ref[...] = jnp.zeros_like(loss_ref)
 
     def columns(tile):
-        return pl.ds(pl.multiple_of(tile * TILE, TILE), TILE)
+        return pl.ds(tile * TILE, TILE)
 
     def multiply(tile, out):
         out[...] = lax.dot_general(
@@ -138,14 +138,11 @@
     own_q = jnp.where(here, own_q, plain_q).astype(BF)
     own_loss = jnp.where(here, own_loss - plain_loss, 0.0)
 
-    def body(pair, carry):
-        multiply(2 * pair + 1, odd)
-        finish(2 * pair, even)
-        multiply(jnp.minimum(2 * pair + 2, tiles - 1), even)
-        finish(2 * pair + 1, odd)
-        return carry
-
-    lax.fori_loop(0, tiles // 2, body, 0)
+    buffers = (even, odd)
+    for tile in range(tiles):
+        if tile + 1 < tiles:
+            multiply(tile + 1, buffers[(tile + 1) % 2])
+        finish(tile, buffers[tile % 2])
     q_ref[:rows, :rows] = own_q
     loss_ref[:rows, :] += own_loss
     half = texts.shape[0] // 2

time: 251 us -> 250 us (level)
  Pallas kernels: 33.9 us -> 31.1 us
  blocking collectives: 74.6 us -> 77.2 us
    pallas_call x1, Pallas kernels: 25.7 us -> 23 us  [pair_call(): pl.pallas_call(functools.partial(pair_kernel, len(images), rows), in_spec...]
    all_to_all x1, blocking collectives: 34.1 us -> 36.6 us  [reduce_weights(): lax.all_to_all(jnp.broadcast_to(total[None], (16,) + total.shape), ('z',...]
where the time goes in v4:
time: 250 us; the launch traced here: 249 us
  blocking collectives  77.2 us (31%)
  waiting for transfers between devices  66.3 us (27%)
  starting transfers between devices  41.9 us (17%)
  Pallas kernels  31.1 us (12%)
  other arithmetic  22.1 us (9%)
  matrix products  4.43 us (2%)
  local copies, waits for them, and re-layouts  3.79 us (2%)
    all_to_all x1, blocking collectives, reduce_weights(): lax.all_to_all(part.astype(BF).reshape(16, rows // 16, cols), ('z', 'x'),...  40.5 us
    all_to_all x1, blocking collectives, reduce_weights(): lax.all_to_all(jnp.broadcast_to(total[None], (16,) + total.shape), ('z',...  36.6 us
    pallas_call x1, Pallas kernels, pair_call(): pl.pallas_call(functools.partial(pair_kernel, len(images), rows), in_spec...  23 us
    all_to_all x1, waiting for transfers between devices, per_device(): lax.all_to_all(img_parts.reshape(8, rows, -1), ('yh', 'x'), 0, 0, tiled=T...  20.5 us
    ppermute x6, waiting for transfers between devices, fetch(): return lax.ppermute(block, axis, [(i, (i - step) % 4) for i in range(4)])  19.8 us
    ppermute x6, waiting for transfers between devices, swap(): return lax.ppermute(block, axis, [(0, 1), (1, 0)])  14.9 us
    ppermute x6, starting transfers between devices, swap(): return lax.ppermute(block, axis, [(0, 1), (1, 0)])  12.2 us
    ppermute x6, starting transfers between devices, fetch(): return lax.ppermute(block, axis, [(i, (i - step) % 4) for i in range(4)])  8.42 us
  transfers between devices with their start and end apart: 20, of which 13 were waited for; matrix products, arithmetic and copies ran while one was open for 3% of the time, Pallas kernels for 3%

profile of v4, /device:TPU:1, one launch (start us, length us, event | category | flops | bytes accessed | tf_op | source)
XLA Modules:
  0.0 249.2 jit_solution(16299653517316420799)
XLA Ops:
  0.6 1.2 convert_reduce_fusion.2
  1.9 1.2 fusion.17
  3.6 1.2 fusion.4
  6.2 3.8 %collective-permute-start = (bf16[128,1152]{1,0:T(8,128)(2,1)S(1)}, bf16[128,1152]{1,0:T(8,128)(2,1)}, u32[]{:S(2)}, u32[]{:S(2)}) collective-permute-start(bf16[128,1152]{1,0:T(8,128)(2,1)S(1)} %multiply_convert_fusion.1.refs_0_), channel_id=1, source_target_pairs={{0,4},{4,0},{1,5},{5,1},{2,6},{6,2},{3,7},{7,3},{8,12},{12,8},{9,1... | collective-permute-start | bytes 884744 | tf_op jit(solution)/shard_map/ppermute | solution.py:53
  13.0 3.5 %collective-permute-done.refs_4_ = bf16[128,1152]{1,0:T(8,128)(2,1)} collective-permute-done((bf16[128,1152]{1,0:T(8,128)(2,1)S(1)}, bf16[128,1152]{1,0:T(8,128)(2,1)}, u32[]{:S(2)}, u32[]{:S(2)}) %collective-permute-start) | collective-permute-done | bytes 294944 | tf_op jit(solution)/shard_map/ppermute | solution.py:53
  16.6 1.7 broadcast_in_dim.4
  18.3 6.0 %all-to-all-start = ((bf16[8,128,1152]{2,1,0:T(8,128)(2,1)}), bf16[8,128,1152]{2,1,0:T(8,128)(2,1)}, u32[]{:S(2)}, u32[]{:S(2)}) async-start(bf16[8,128,1152]{2,1,0:T(8,128)(2,1)} %broadcast_in_dim.4), calls=%async_computation | async-start | bytes 4718592 | tf_op jit(solution)/shard_map/all_to_all | solution.py:270
  24.3 1.2 collective-permute-start.3
  25.6 1.4 collective-permute-start.2
  27.0 1.5 collective-permute-start.1
  28.9 2.4 collective-permute-start.5
  31.2 1.3 collective-permute-done.3.refs_3_
  32.5 1.5 collective-permute-start.4
  34.1 5.8 %collective-permute-done.1.refs_1_ = bf16[128,1152]{1,0:T(8,128)(2,1)} collective-permute-done((bf16[128,1152]{1,0:T(8,128)(2,1)}, bf16[128,1152]{1,0:T(8,128)(2,1)}, u32[]{:S(2)}, u32[]{:S(2)}) %collective-permute-start.1) | collective-permute-done | bytes 294944 | tf_op jit(solution)/shard_map/ppermute | solution.py:45
  39.9 5.6 %collective-permute-done.6.refs_7_ = bf16[128,1152]{1,0:T(8,128)(2,1)} collective-permute-done((bf16[128,1152]{1,0:T(8,128)(2,1)}, bf16[128,1152]{1,0:T(8,128)(2,1)}, u32[]{:S(2)}, u32[]{:S(2)}) %collective-permute-start.6) | collective-permute-done | bytes 294944 | tf_op jit(solution)/shard_map/ppermute | solution.py:45
  45.5 7.0 %collective-permute-done.4.refs_5_ = bf16[128,1152]{1,0:T(8,128)(2,1)} collective-permute-done((bf16[128,1152]{1,0:T(8,128)(2,1)}, bf16[128,1152]{1,0:T(8,128)(2,1)}, u32[]{:S(2)}, u32[]{:S(2)}) %collective-permute-start.4) | collective-permute-done | bytes 294944 | tf_op jit(solution)/shard_map/ppermute | solution.py:45
  52.5 0.9 all-to-all-done
  53.4 1.9 collective-permute-start.7
  56.7 3.0 %collective-permute-done.7.refs_9_ = bf16[1024,1152]{1,0:T(8,128)(2,1)} collective-permute-done((bf16[1024,1152]{1,0:T(8,128)(2,1)}, bf16[1024,1152]{1,0:T(8,128)(2,1)}, u32[]{:S(2)}, u32[]{:S(2)}) %collective-permute-start.7) | collective-permute-done | bytes 2359328 | tf_op jit(solution)/shard_map/ppermute | solution.py:53
  59.8 23.0 %pair.1 = (bf16[1024,1152]{1,0:T(8,128)(2,1)}, bf16[1024,1024]{1,0:T(8,128)(2,1)}, bf16[1024,1280]{1,0:T(8,128)(2,1)}) custom-call(bf16[128,1152]{1,0:T(8,128)(2,1)} %copy-done.16, bf16[128,1152]{1,0:T(8,128)(2,1)} %collective-permute-done.1.refs_1_, bf16[128,1152]{1,0:T(8,128)(2,1)} %collective-permute-done.2.refs_2_, ...), custom_call_target="tpu_custom_call" | custom-call | flops 14495514624 | bytes 16777216 | tf_op jit(solution)/shard_map/pair/pallas_call | solution.py:171
  83.3 5.3 %all-to-all-start.1 = ((bf16[8,128,1280]{2,1,0:T(8,128)(2,1)}), bf16[8,128,1280]{2,1,0:T(8,128)(2,1)}, u32[]{:S(2)}, u32[]{:S(2)}) async-start(bf16[8,128,1280]{2,1,0:T(8,128)(2,1)} %bitcast.32), calls=%async_computation.1 | async-start | bytes 5242880 | tf_op jit(solution)/shard_map/all_to_all | solution.py:304
  88.6 8.1 %grad_txt.1 = (bf16[256,1152]{1,0:T(8,128)(2,1)}, bf16[256,1152]{1,0:T(8,128)(2,1)}, bf16[256,1152]{1,0:T(8,128)(2,1)}, f32[256,1152]{1,0:T(8,128)}) custom-call(bf16[1024,1024]{1,0:T(8,128)(2,1)} %get-tuple-element.40.q_ref, bf16[128,1152]{1,0:T(8,128)(2,1)} %copy-done.16, bf16[128,1152]{1,0:T(8,128)(2,1)} %collective-permute-done.1.refs_1_, ...), custom_call_target="tpu_custom_call" | custom-call | flops 2415919104 | bytes 6291456 | tf_op jit(solution)/shard_map/grad_txt/pallas_call | solution.py:229
  96.7 3.0 %collective-permute-start.9 = (bf16[256,1152]{1,0:T(8,128)(2,1)}, bf16[256,1152]{1,0:T(8,128)(2,1)}, u32[]{:S(2)}, u32[]{:S(2)}) collective-permute-start(bf16[256,1152]{1,0:T(8,128)(2,1)} %get-tuple-element.42), channel_id=1, source_target_pairs={{0,32},{16,48},{32,0},{48,16},{1,33},{17,49},{33,1},{49,17},{2,34}... | collective-permute-start | bytes 1769480 | tf_op jit(solution)/shard_map/ppermute | solution.py:49
  100.0 2.4 collective-permute-start.11
  102.4 20.5 %all-to-all-done.1 = bf16[8,128,1280]{2,1,0:T(8,128)(2,1)} async-done(((bf16[8,128,1280]{2,1,0:T(8,128)(2,1)}), bf16[8,128,1280]{2,1,0:T(8,128)(2,1)}, u32[]{:S(2)}, u32[]{:S(2)}) %all-to-all-start.1) | async-done | bytes 2621472 | tf_op jit(solution)/shard_map/all_to_all | solution.py:304
  122.9 3.6 %collective-permute-done.10 = bf16[256,1152]{1,0:T(8,128)(2,1)} collective-permute-done((bf16[256,1152]{1,0:T(8,128)(2,1)}, bf16[256,1152]{1,0:T(8,128)(2,1)}, u32[]{:S(2)}, u32[]{:S(2)}) %collective-permute-start.10) | collective-permute-done | bytes 589856 | tf_op jit(solution)/shard_map/ppermute | solution.py:49
  126.5 2.2 convert_reduce_fusion
  128.9 1.8 add_add_fusion
  130.8 0.9 collective-permute-start.12
  131.9 6.8 %collective-permute-done.12 = bf16[128,1152]{1,0:T(8,128)(2,1)S(1)} collective-permute-done((bf16[128,1152]{1,0:T(8,128)(2,1)S(1)}, bf16[128,1152]{1,0:T(8,128)(2,1)S(1)}, u32[]{:S(2)}, u32[]{:S(2)}) %collective-permute-start.12) | collective-permute-done | bytes 294944 | tf_op jit(solution)/shard_map/ppermute | solution.py:53
  139.2 1.7 collective-permute-start.13
  141.0 1.6 collective-permute-done.13
  142.6 1.0 convolution_convert_fusion
  143.6 40.5 %all_to_all.20 = bf16[16,72,1152]{2,1,0:T(8,128)(2,1)} all-to-all(bf16[16,72,1152]{2,1,0:T(8,128)(2,1)S(1)} %bitcast.31), channel_id=1, replica_groups=mesh['yl'=2,'z'=4,'c'=2,'yh'=2,'x'=4] {'z','x'}, dimensions={0} | all-to-all | bytes 5308416 | tf_op jit(solution)/shard_map/all_to_all | solution.py:275
  184.2 2.2 reduce_sum.152
  186.3 2.8 %collective-permute-start.16 = (bf16[72,1152]{1,0:T(8,128)(2,1)S(1)}, bf16[72,1152]{1,0:T(8,128)(2,1)S(1)}, u32[]{:S(2)}, u32[]{:S(2)}) collective-permute-start(bf16[72,1152]{1,0:T(8,128)(2,1)S(1)} %reduce_sum.152), channel_id=1, source_target_pairs={{0,68},{64,0},{4,64},{68,4},{1,69},{65,1},{5,65},{69,5},{2,70},{66... | collective-permute-start | bytes 497672 | tf_op jit(solution)/shard_map/ppermute | solution.py:279
  189.1 1.5 collective-permute-start.14
  190.6 0.8 collective-permute-done.16
  191.4 5.8 %collective-permute-done.15 = bf16[72,1152]{1,0:T(8,128)(2,1)S(1)} collective-permute-done((bf16[72,1152]{1,0:T(8,128)(2,1)S(1)}, bf16[72,1152]{1,0:T(8,128)(2,1)S(1)}, u32[]{:S(2)}, u32[]{:S(2)}) %collective-permute-start.15) | collective-permute-done | bytes 165920 | tf_op jit(solution)/shard_map/ppermute | solution.py:279
  197.2 1.0 add_convert_fusion
  198.4 36.6 %all_to_all.21 = bf16[16,72,1152]{2,1,0:T(8,128)(2,1)S(1)} all-to-all(bf16[16,72,1152]{2,1,0:T(8,128)(2,1)S(1)} %broadcast_in_dim.5), channel_id=1, replica_groups=mesh['yl'=2,'z'=4,'c'=2,'yh'=2,'x'=4] {'z','x'}, dimensions={0} | all-to-all | bytes 5308416 | tf_op jit(solution)/shard_map/all_to_all | solution.py:281
  235.1 3.4 %collective-permute-start.17 = (bf16[1152,1152]{1,0:T(8,128)(2,1)S(1)}, bf16[1152,1152]{1,0:T(8,128)(2,1)S(1)}, u32[]{:S(2)}, u32[]{:S(2)}) collective-permute-start(bf16[1152,1152]{1,0:T(8,128)(2,1)S(1)} %bitcast.30), channel_id=1, source_target_pairs={{0,8},{8,0},{1,9},{9,1},{2,10},{10,2},{3,11},{11,3},{4,12},{12,4},... | collective-permute-start | bytes 7962632 | tf_op jit(solution)/shard_map/ppermute | solution.py:53
  238.5 0.9 slice_reduce_fusion
  240.0 1.0 fusion.26
  241.0 1.1 fusion.16
  242.1 1.0 fusion.25
  243.1 1.1 fusion.12
  244.2 5.0 %select_convert_fusion = (f32[1152,1152]{1,0:T(8,128)}, f32[1152,1152]{1,0:T(8,128)}) fusion(bf16[1152,1152]{1,0:T(8,128)(2,1)S(1)} %collective-permute-done.17, pred[]{:T(512)S(6)} %eq.23, bf16[16,72,1152]{2,1,0:T(8,128)(2,1)S(1)} %all_to_all.21), kind=kLoop, calls=%fused_computation.2 | loop fusion | flops 5308416 | bytes 15925249 | tf_op jit(solution)/shard_map/convert_element_type | solution.py:324
  (92 shorter events, 7.9 us)
Async XLA Ops:
  0.6 4.2 %copy-start = (bf16[1152,1152]{1,0:T(8,128)(2,1)S(1)}, bf16[1152,1152]{1,0:T(8,128)(2,1)}, u32[]{:S(2)}) copy-start(bf16[1152,1152]{1,0:T(8,128)(2,1)} %param.8) | copy-start | bytes 7962628
  1.9 8.1 %copy-start.6 = (bf16[128,1152]{1,0:T(8,128)(2,1)S(1)}, bf16[128,1152]{1,0:T(8,128)(2,1)}, u32[]{:S(2)}) copy-start(bf16[128,1152]{1,0:T(8,128)(2,1)} %param.7) | copy-start | bytes 884740
  3.1 0.5 copy-start.17
  4.8 5.6 %copy-start.10 = (bf16[128,1152]{1,0:T(8,128)(2,1)}, bf16[128,1152]{1,0:T(8,128)(2,1)S(1)}, u32[]{:S(2)}) copy-start(bf16[128,1152]{1,0:T(8,128)(2,1)S(1)} %fusion.4) | copy-start | bytes 884740
  4.8 6.3 %copy-start.1 = (bf16[1152,1152]{1,0:T(8,128)(2,1)S(1)}, bf16[1152,1152]{1,0:T(8,128)(2,1)}, u32[]{:S(2)}) copy-start(bf16[1152,1152]{1,0:T(8,128)(2,1)} %param.9) | copy-start | bytes 7962628
  6.1 4.3 %copy-start.21 = (f32[128]{0:T(128)}, f32[128]{0:T(128)S(1)}, u32[]{:S(2)}) copy-start(f32[128]{0:T(128)S(1)} %get-tuple-element.66) | copy-start | bytes 1540
  6.2 6.6 %copy-start.16 = (bf16[128,1152]{1,0:T(8,128)(2,1)}, bf16[128,1152]{1,0:T(8,128)(2,1)S(1)}, u32[]{:S(2)}) copy-start(bf16[128,1152]{1,0:T(8,128)(2,1)S(1)} %multiply_convert_fusion.1.refs_0_) | copy-start | bytes 884740
  6.2 10.4 %collective-permute-start = (bf16[128,1152]{1,0:T(8,128)(2,1)S(1)}, bf16[128,1152]{1,0:T(8,128)(2,1)}, u32[]{:S(2)}, u32[]{:S(2)}) collective-permute-start(bf16[128,1152]{1,0:T(8,128)(2,1)S(1)} %multiply_convert_fusion.1.refs_0_), channel_id=1, source_target_pairs={{0,4},{4,0},{1,5},{5,1},{2,6},{6,2},{3,7},{7,3},{8,12},{12,8},{9,1... | collective-permute-start | bytes 884744 | tf_op jit(solution)/shard_map/ppermute | solution.py:53
  10.4 0.5 copy-start.19
  11.2 1.6 copy-start.12
  11.9 0.8 copy-start.3
  12.5 0.6 copy-start.23
  18.3 35.1 %all-to-all-start = ((bf16[8,128,1152]{2,1,0:T(8,128)(2,1)}), bf16[8,128,1152]{2,1,0:T(8,128)(2,1)}, u32[]{:S(2)}, u32[]{:S(2)}) async-start(bf16[8,128,1152]{2,1,0:T(8,128)(2,1)} %broadcast_in_dim.4), calls=%async_computation | async-start | bytes 4718592 | tf_op jit(solution)/shard_map/all_to_all | solution.py:270
  24.3 8.2 %collective-permute-start.3 = (bf16[128,1152]{1,0:T(8,128)(2,1)}, bf16[128,1152]{1,0:T(8,128)(2,1)}, u32[]{:S(2)}, u32[]{:S(2)}) collective-permute-start(bf16[128,1152]{1,0:T(8,128)(2,1)} %copy-done.16), channel_id=1, source_target_pairs={{0,1},{1,2},{2,3},{3,0},{4,5},{5,6},{6,7},{7,4},{8,9},{9,10},{10,1... | collective-permute-start | bytes 884744 | tf_op jit(solution)/shard_map/ppermute | solution.py:45
  25.6 8.5 %collective-permute-start.2 = (bf16[128,1152]{1,0:T(8,128)(2,1)}, bf16[128,1152]{1,0:T(8,128)(2,1)}, u32[]{:S(2)}, u32[]{:S(2)}) collective-permute-start(bf16[128,1152]{1,0:T(8,128)(2,1)} %copy-done.16), channel_id=1, source_target_pairs={{0,3},{1,0},{2,1},{3,2},{4,7},{5,4},{6,5},{7,6},{8,11},{9,8},{10,9... | collective-permute-start | bytes 884744 | tf_op jit(solution)/shard_map/ppermute | solution.py:45
  27.0 12.9 %collective-permute-start.1 = (bf16[128,1152]{1,0:T(8,128)(2,1)}, bf16[128,1152]{1,0:T(8,128)(2,1)}, u32[]{:S(2)}, u32[]{:S(2)}) collective-permute-start(bf16[128,1152]{1,0:T(8,128)(2,1)} %copy-done.16), channel_id=1, source_target_pairs={{0,2},{1,3},{2,0},{3,1},{4,6},{5,7},{6,4},{7,5},{8,10},{9,11},{10,... | collective-permute-start | bytes 884744 | tf_op jit(solution)/shard_map/ppermute | solution.py:45
  28.5 16.9 %collective-permute-start.6 = (bf16[128,1152]{1,0:T(8,128)(2,1)}, bf16[128,1152]{1,0:T(8,128)(2,1)}, u32[]{:S(2)}, u32[]{:S(2)}) collective-permute-start(bf16[128,1152]{1,0:T(8,128)(2,1)} %collective-permute-done.refs_4_), channel_id=1, source_target_pairs={{0,1},{1,2},{2,3},{3,0},{4,5},{5,6},{6,7},{7,4},{8,9},{9,10},{10,1... | collective-permute-start | bytes 884744 | tf_op jit(solution)/shard_map/ppermute | solution.py:45
  28.9 16.6 %collective-permute-start.5 = (bf16[128,1152]{1,0:T(8,128)(2,1)}, bf16[128,1152]{1,0:T(8,128)(2,1)}, u32[]{:S(2)}, u32[]{:S(2)}) collective-permute-start(bf16[128,1152]{1,0:T(8,128)(2,1)} %collective-permute-done.refs_4_), channel_id=1, source_target_pairs={{0,3},{1,0},{2,1},{3,2},{4,7},{5,4},{6,5},{7,6},{8,11},{9,8},{10,9... | collective-permute-start | bytes 884744 | tf_op jit(solution)/shard_map/ppermute | solution.py:45
  32.5 20.0 %collective-permute-start.4 = (bf16[128,1152]{1,0:T(8,128)(2,1)}, bf16[128,1152]{1,0:T(8,128)(2,1)}, u32[]{:S(2)}, u32[]{:S(2)}) collective-permute-start(bf16[128,1152]{1,0:T(8,128)(2,1)} %collective-permute-done.refs_4_), channel_id=1, source_target_pairs={{0,2},{1,3},{2,0},{3,1},{4,6},{5,7},{6,4},{7,5},{8,10},{9,11},{10,... | collective-permute-start | bytes 884744 | tf_op jit(solution)/shard_map/ppermute | solution.py:45
  53.4 6.4 %collective-permute-start.7 = (bf16[1024,1152]{1,0:T(8,128)(2,1)}, bf16[1024,1152]{1,0:T(8,128)(2,1)}, u32[]{:S(2)}, u32[]{:S(2)}) collective-permute-start(bf16[1024,1152]{1,0:T(8,128)(2,1)} %bitcast.refs_8_), channel_id=1, source_target_pairs={{0,8},{8,0},{1,9},{9,1},{2,10},{10,2},{3,11},{11,3},{4,12},{12,4},... | collective-permute-start | bytes 7077896 | tf_op jit(solution)/shard_map/ppermute | solution.py:53
  82.8 5.8 %collective-permute-start.8 = (bf16[1024,1152]{1,0:T(8,128)(2,1)}, bf16[1024,1152]{1,0:T(8,128)(2,1)}, u32[]{:S(2)}, u32[]{:S(2)}) collective-permute-start(bf16[1024,1152]{1,0:T(8,128)(2,1)} %get-tuple-element.41), channel_id=1, source_target_pairs={{0,8},{8,0},{1,9},{9,1},{2,10},{10,2},{3,11},{11,3},{4,12},{12,4},... | collective-permute-start | bytes 7077896 | tf_op jit(solution)/shard_map/ppermute | solution.py:53
  83.3 39.7 %all-to-all-start.1 = ((bf16[8,128,1280]{2,1,0:T(8,128)(2,1)}), bf16[8,128,1280]{2,1,0:T(8,128)(2,1)}, u32[]{:S(2)}, u32[]{:S(2)}) async-start(bf16[8,128,1280]{2,1,0:T(8,128)(2,1)} %bitcast.32), calls=%async_computation.1 | async-start | bytes 5242880 | tf_op jit(solution)/shard_map/all_to_all | solution.py:304
  96.7 26.2 %collective-permute-start.9 = (bf16[256,1152]{1,0:T(8,128)(2,1)}, bf16[256,1152]{1,0:T(8,128)(2,1)}, u32[]{:S(2)}, u32[]{:S(2)}) collective-permute-start(bf16[256,1152]{1,0:T(8,128)(2,1)} %get-tuple-element.42), channel_id=1, source_target_pairs={{0,32},{16,48},{32,0},{48,16},{1,33},{17,49},{33,1},{49,17},{2,34}... | collective-permute-start | bytes 1769480 | tf_op jit(solution)/shard_map/ppermute | solution.py:49
  99.7 26.8 %collective-permute-start.10 = (bf16[256,1152]{1,0:T(8,128)(2,1)}, bf16[256,1152]{1,0:T(8,128)(2,1)}, u32[]{:S(2)}, u32[]{:S(2)}) collective-permute-start(bf16[256,1152]{1,0:T(8,128)(2,1)} %get-tuple-element.43), channel_id=1, source_target_pairs={{0,16},{16,32},{32,48},{48,0},{1,17},{17,33},{33,49},{49,1},{2,18}... | collective-permute-start | bytes 1769480 | tf_op jit(solution)/shard_map/ppermute | solution.py:49
  100.0 26.5 %collective-permute-start.11 = (bf16[256,1152]{1,0:T(8,128)(2,1)}, bf16[256,1152]{1,0:T(8,128)(2,1)}, u32[]{:S(2)}, u32[]{:S(2)}) collective-permute-start(bf16[256,1152]{1,0:T(8,128)(2,1)} %get-tuple-element.44), channel_id=1, source_target_pairs={{0,48},{16,0},{32,16},{48,32},{1,49},{17,1},{33,17},{49,33},{2,50}... | collective-permute-start | bytes 1769480 | tf_op jit(solution)/shard_map/ppermute | solution.py:49
  122.9 6.0 %copy-start.14 = (f32[256,1152]{1,0:T(8,128)S(1)}, f32[256,1152]{1,0:T(8,128)}, u32[]{:S(2)}) copy-start(f32[256,1152]{1,0:T(8,128)} %get-tuple-element.50) | copy-start | bytes 3538948
  128.7 3.0 %copy-start.7 = (f32[128,1280]{1,0:T(8,128)}, f32[128,1280]{1,0:T(8,128)S(1)}, u32[]{:S(2)}) copy-start(f32[128,1280]{1,0:T(8,128)S(1)} %convert_reduce_fusion) | copy-start | bytes 1966084
  128.9 2.8 %copy-start.22 = (f32[128]{0:T(128)S(1)}, f32[128]{0:T(128)}, u32[]{:S(2)}) copy-start(f32[128]{0:T(128)} %copy-done.21) | copy-start | bytes 1540
  128.9 2.8 %copy-start.25 = (f32[128]{0:T(128)S(1)}, f32[128]{0:T(128)}, u32[]{:S(2)}) copy-start(f32[128]{0:T(128)} %get-tuple-element.65) | copy-start | bytes 1540
  128.9 9.7 %copy-start.4 = (f32[128,1152]{1,0:T(8,128)S(1)}, f32[128,1152]{1,0:T(8,128)}, u32[]{:S(2)}) copy-start(f32[128,1152]{1,0:T(8,128)} %copy-done.3) | copy-start | bytes 1769476
  130.7 8.1 %copy-start.24 = (f32[128]{0:T(128)S(1)}, f32[128]{0:T(128)}, u32[]{:S(2)}) copy-start(f32[128]{0:T(128)} %copy-done.23) | copy-start | bytes 1540
  130.7 8.1 %copy-start.26 = (f32[128]{0:T(128)S(1)}, f32[128]{0:T(128)}, u32[]{:S(2)}) copy-start(f32[128]{0:T(128)} %get-tuple-element.63) | copy-start | bytes 1540
  130.7 8.3 %copy-start.11 = (bf16[128,1152]{1,0:T(8,128)(2,1)S(1)}, bf16[128,1152]{1,0:T(8,128)(2,1)}, u32[]{:S(2)}) copy-start(bf16[128,1152]{1,0:T(8,128)(2,1)} %copy-done.10) | copy-start | bytes 884740
  130.7 8.3 %copy-start.13 = (bf16[128,1152]{1,0:T(8,128)(2,1)S(1)}, bf16[128,1152]{1,0:T(8,128)(2,1)}, u32[]{:S(2)}) copy-start(bf16[128,1152]{1,0:T(8,128)(2,1)} %copy-done.12) | copy-start | bytes 884740
  130.8 7.9 %collective-permute-start.12 = (bf16[128,1152]{1,0:T(8,128)(2,1)S(1)}, bf16[128,1152]{1,0:T(8,128)(2,1)S(1)}, u32[]{:S(2)}, u32[]{:S(2)}) collective-permute-start(bf16[128,1152]{1,0:T(8,128)(2,1)S(1)} %slice.50), channel_id=1, source_target_pairs={{0,64},{64,0},{1,65},{65,1},{2,66},{66,2},{3,67},{67,3},{4,68},{68... | collective-permute-start | bytes 884744 | tf_op jit(solution)/shard_map/ppermute | solution.py:53
  131.9 7.4 %copy-start.8 = (bf16[128,1152]{1,0:T(8,128)(2,1)}, bf16[128,1152]{1,0:T(8,128)(2,1)S(1)}, u32[]{:S(2)}) copy-start(bf16[128,1152]{1,0:T(8,128)(2,1)S(1)} %subtract_convert_fusion.1) | copy-start | bytes 884740
  139.2 3.4 %collective-permute-start.13 = (bf16[256,1152]{1,0:T(8,128)(2,1)S(1)}, bf16[256,1152]{1,0:T(8,128)(2,1)S(1)}, u32[]{:S(2)}, u32[]{:S(2)}) collective-permute-start(bf16[256,1152]{1,0:T(8,128)(2,1)S(1)} %get-tuple-element.58), channel_id=1, source_target_pairs={{0,8},{8,0},{1,9},{9,1},{2,10},{10,2},{3,11},{11,3},{4,12},{12,4},... | collective-permute-start | bytes 1769480 | tf_op jit(solution)/shard_map/ppermute | solution.py:53
  186.3 10.9 %copy-start.15 = (bf16[72,1152]{1,0:T(8,128)(2,1)}, bf16[72,1152]{1,0:T(8,128)(2,1)S(1)}, u32[]{:S(2)}) copy-start(bf16[72,1152]{1,0:T(8,128)(2,1)S(1)} %reduce_sum.152) | copy-start | bytes 497668
  186.3 5.0 %collective-permute-start.16 = (bf16[72,1152]{1,0:T(8,128)(2,1)S(1)}, bf16[72,1152]{1,0:T(8,128)(2,1)S(1)}, u32[]{:S(2)}, u32[]{:S(2)}) collective-permute-start(bf16[72,1152]{1,0:T(8,128)(2,1)S(1)} %reduce_sum.152), channel_id=1, source_target_pairs={{0,68},{64,0},{4,64},{68,4},{1,69},{65,1},{5,65},{69,5},{2,70},{66... | collective-permute-start | bytes 497672 | tf_op jit(solution)/shard_map/ppermute | solution.py:279
  189.1 8.1 %collective-permute-start.15 = (bf16[72,1152]{1,0:T(8,128)(2,1)S(1)}, bf16[72,1152]{1,0:T(8,128)(2,1)S(1)}, u32[]{:S(2)}, u32[]{:S(2)}) collective-permute-start(bf16[72,1152]{1,0:T(8,128)(2,1)S(1)} %reduce_sum.152), channel_id=1, source_target_pairs={{0,64},{64,4},{4,68},{68,0},{1,65},{65,5},{5,69},{69,1},{2,66},{66... | collective-permute-start | bytes 497672 | tf_op jit(solution)/shard_map/ppermute | solution.py:279
  189.1 8.1 %collective-permute-start.14 = (bf16[72,1152]{1,0:T(8,128)(2,1)S(1)}, bf16[72,1152]{1,0:T(8,128)(2,1)S(1)}, u32[]{:S(2)}, u32[]{:S(2)}) collective-permute-start(bf16[72,1152]{1,0:T(8,128)(2,1)S(1)} %reduce_sum.152), channel_id=1, source_target_pairs={{0,4},{64,68},{4,0},{68,64},{1,5},{65,69},{5,1},{69,65},{2,6},{66,... | collective-permute-start | bytes 497672 | tf_op jit(solution)/shard_map/ppermute | solution.py:279
  198.4 41.5 %copy-start.5 = (bf16[128,1152]{1,0:T(8,128)(2,1)S(1)}, bf16[128,1152]{1,0:T(8,128)(2,1)}, u32[]{:S(2)}) copy-start(bf16[128,1152]{1,0:T(8,128)(2,1)} %param.6) | copy-start | bytes 884740
  198.4 41.5 %copy-start.9 = (bf16[128,1152]{1,0:T(8,128)(2,1)S(1)}, bf16[128,1152]{1,0:T(8,128)(2,1)}, u32[]{:S(2)}) copy-start(bf16[128,1152]{1,0:T(8,128)(2,1)} %copy-done.8) | copy-start | bytes 884740
  198.4 41.5 %copy-start.18 = (f32[128]{0:T(128)S(1)}, f32[128]{0:T(128)}, u32[]{:S(2)}) copy-start(f32[128]{0:T(128)} %copy-done.17) | copy-start | bytes 1540
  235.1 9.1 %collective-permute-start.17 = (bf16[1152,1152]{1,0:T(8,128)(2,1)S(1)}, bf16[1152,1152]{1,0:T(8,128)(2,1)S(1)}, u32[]{:S(2)}, u32[]{:S(2)}) collective-permute-start(bf16[1152,1152]{1,0:T(8,128)(2,1)S(1)} %bitcast.30), channel_id=1, source_target_pairs={{0,8},{8,0},{1,9},{9,1},{2,10},{10,2},{3,11},{11,3},{4,12},{12,4},... | collective-permute-start | bytes 7962632 | tf_op jit(solution)/shard_map/ppermute | solution.py:53
  239.9 2.1 copy-start.2
  239.9 2.1 copy-start.20
